TPU v7x, 512 devices: a whole 4x4x16 slice. The times are simulated.
512 devices in a mesh: dp: 32 (over x, z_hi, core), group: 16 (over z_lo, y).
Axes of the slice: x: 4, y: 4, z: 16 (z_hi: 4, z_lo: 4; z = z_hi * 4 + z_lo), core: 2. Of those that a mesh axis runs over, the one named last changes fastest.
Arguments:
- tokens: bfloat16 [2048, 32, 4096], P(('dp', 'group')), may hold values from -40 to 40
- grad_out: bfloat16 [2048, 32, 4096], P(('dp', 'group')), may hold values from -6 to 6
- members: int32 [32, 64], P('dp'), may hold values from 0 to 63, each once within a row
- router: bfloat16 [4096, 1], replicated, may hold values from -1 to 1
- w_in: bfloat16 [1, 4096, 2048], P(None, 'dp', 'group'), may hold values from -0.09375 to 0.09375
- w_out: bfloat16 [1, 2048, 4096], P(None, 'group', 'dp'), may hold values from -0.125 to 0.125
Outputs:
- grad_tokens: bfloat16 [2048, 32, 4096], P(('dp', 'group'))
- grad_w_in: bfloat16 [1, 4096, 2048], P(None, 'dp', 'group')
- grad_w_out: bfloat16 [1, 2048, 4096], P(None, 'group', 'dp')
- grad_router: float32 [4096, 1], replicated
Inputs may be any that keep to these rules, and one draw needn't show every extreme that they name: Each row of members holds every number below 64 once.
All inputs are finite; a program needn't handle non-finite values.
Results may differ from a plain program's by a relative error of at most 0.03.
Values may be sent and summed in bfloat16 or wider, within the bound.
No kernel may reach another device: no remote copies, remote signals or barrier semaphores. Data moves between devices by JAX's collectives and lax.ppermute only.
A program may use at most 64 MiB of HBM per device.

v0:
```python
import jax
import jax.numpy as jnp
from jax import lax
from jax.sharding import PartitionSpec as P

GSIZE = 32


def silu_slope(values):
    sigma = jax.nn.sigmoid(values)
    return sigma * (1.0 + values * (1.0 - sigma))


def shards(tokens, grad_out, members, router, w_in, w_out):
    seq_row = members.shape[1]
    width = tokens.shape[2]
    experts = router.shape[1]
    clusters = seq_row // GSIZE
    order = members[0]
    inverse = jnp.zeros((seq_row,), jnp.int32).at[order].set(jnp.arange(seq_row, dtype=jnp.int32))
    token_rows, grad_rows = (
        lax.all_to_all(tokens, "group", split_axis=1, concat_axis=0, tiled=True),
        lax.all_to_all(grad_out, "group", split_axis=1, concat_axis=0, tiled=True),
    )
    places = token_rows.shape[1]
    token_grp = jnp.take(token_rows, order, axis=0).reshape(clusters, GSIZE, places, width)
    grad_grp = jnp.take(grad_rows, order, axis=0).reshape(clusters, GSIZE, places, width)
    logits = jnp.einsum("kipd,de->kipe", token_grp, router, preferred_element_type=jnp.float32)
    weights = jax.nn.softmax(logits, axis=1)
    weights_b = weights.astype(jnp.bfloat16)
    mixed = jnp.einsum(
        "kipe,kipd->pked", weights_b, token_grp, preferred_element_type=jnp.float32
    ).astype(jnp.bfloat16)
    dmix_out = jnp.einsum(
        "kipe,kipd->pked", weights_b, grad_grp, preferred_element_type=jnp.float32
    ).astype(jnp.bfloat16)
    local_rows = places * clusters
    all_mixed, all_dout = (
        lax.all_gather(mixed.reshape(local_rows, experts, width), "group", axis=0, tiled=True),
        lax.all_gather(dmix_out.reshape(local_rows, experts, width), "group", axis=0, tiled=True),
    )
    full_in, full_out = (
        lax.all_gather(w_in, "dp", axis=1, tiled=True),
        lax.all_gather(w_out, "dp", axis=2, tiled=True),
    )
    hidden = jnp.einsum("red,edf->ref", all_mixed, full_in, preferred_element_type=jnp.float32)
    active = jax.nn.silu(hidden).astype(jnp.bfloat16)
    out_terms = jnp.einsum("ref,efd->red", active, full_out, preferred_element_type=jnp.float32)
    d_act = jnp.einsum("red,efd->ref", all_dout, full_out, preferred_element_type=jnp.float32)
    d_pre = (d_act * silu_slope(hidden)).astype(jnp.bfloat16)
    back_terms = jnp.einsum("ref,edf->red", d_pre, full_in, preferred_element_type=jnp.float32)
    expert_rows = lax.psum_scatter(
        out_terms.astype(jnp.bfloat16), "group", scatter_dimension=0, tiled=True
    )
    part_out = jnp.einsum("ref,red->efd", active, all_dout, preferred_element_type=jnp.float32)
    part_in = jnp.einsum("red,ref->edf", all_mixed, d_pre, preferred_element_type=jnp.float32)
    grad_in, grad_outer = (
        lax.psum_scatter(
            part_in.astype(jnp.bfloat16), "dp", scatter_dimension=1, tiled=True
        ).astype(jnp.float32),
        lax.psum_scatter(
            part_out.astype(jnp.bfloat16), "dp", scatter_dimension=2, tiled=True
        ).astype(jnp.float32),
    )
    dmixed_rows = lax.psum_scatter(
        back_terms.astype(jnp.bfloat16), "group", scatter_dimension=0, tiled=True
    )
    expert_out = expert_rows.reshape(places, clusters, experts, width)
    dmixed = dmixed_rows.reshape(places, clusters, experts, width)
    d_mix = jnp.einsum("kipd,pked->kipe", grad_grp, expert_out, preferred_element_type=jnp.float32)
    d_mix = d_mix + jnp.einsum(
        "kipd,pked->kipe", token_grp, dmixed, preferred_element_type=jnp.float32
    )
    centre = jnp.sum(weights * d_mix, axis=1, keepdims=True)
    d_logit = (weights * (d_mix - centre)).astype(jnp.bfloat16)
    d_tok = jnp.einsum("kipe,pked->kipd", weights_b, dmixed, preferred_element_type=jnp.float32)
    d_tok = d_tok + jnp.einsum("kipe,de->kipd", d_logit, router, preferred_element_type=jnp.float32)
    d_tok = d_tok.astype(jnp.bfloat16).reshape(seq_row, places, width)
    d_route = jnp.einsum("kipd,kipe->de", token_grp, d_logit, preferred_element_type=jnp.float32)
    seq_major = jnp.take(d_tok, inverse, axis=0)
    grad_tokens = lax.all_to_all(seq_major, "group", split_axis=0, concat_axis=1, tiled=True)
    grad_router = lax.psum(d_route, ("dp", "group"))
    return (grad_tokens, grad_in.astype(jnp.bfloat16), grad_outer.astype(jnp.bfloat16), grad_router)


def solution(mesh):
    placed = (
        P(("dp", "group"), None, None),
        P(("dp", "group"), None, None),
        P("dp", None),
        P(),
        P(None, "dp", "group"),
        P(None, "group", "dp"),
    )
    return jax.shard_map(
        shards,
        mesh=mesh,
        in_specs=placed,
        out_specs=(
            P(("dp", "group"), None, None),
            P(None, "dp", "group"),
            P(None, "group", "dp"),
            P(),
        ),
        check_vma=False,
    )
```

profile of v0, /device:TPU:1, one launch (start us, length us, event | category | flops | bytes accessed | tf_op | source)
XLA Modules:
  0.0 629.7 jit_solution(5723652784087922712)
XLA Ops:
  7.2 3.1 copy.36
  10.3 9.2 %all-to-all-start = ((bf16[4,32,4096]{2,0,1:T(4,128)(2,1)}), bf16[4,32,4096]{2,0,1:T(4,128)(2,1)S(1)}, u32[]{:S(2)}, u32[]{:S(2)}) async-start(bf16[4,32,4096]{2,0,1:T(4,128)(2,1)} %copy.36), calls=%async_computation | async-start | bytes 2097152 | tf_op jit(solution)/shard_map/all_to_all | solution.py:22
  19.5 1.8 copy.38
  21.3 20.3 %all-to-all-done = bf16[4,32,4096]{2,0,1:T(4,128)(2,1)S(1)} async-done(((bf16[4,32,4096]{2,0,1:T(4,128)(2,1)}), bf16[4,32,4096]{2,0,1:T(4,128)(2,1)S(1)}, u32[]{:S(2)}, u32[]{:S(2)}) %all-to-all-start) | async-done | bytes 1048608 | tf_op jit(solution)/shard_map/all_to_all | solution.py:22
  41.5 7.8 %all-to-all-start.1 = ((bf16[4,32,4096]{2,0,1:T(4,128)(2,1)}), bf16[4,32,4096]{2,0,1:T(4,128)(2,1)S(1)}, u32[]{:S(2)}, u32[]{:S(2)}) async-start(bf16[4,32,4096]{2,0,1:T(4,128)(2,1)} %copy.38), calls=%async_computation.1 | async-start | bytes 2097152 | tf_op jit(solution)/shard_map/all_to_all | solution.py:23
  52.2 19.2 %all-to-all-done.1 = bf16[4,32,4096]{2,0,1:T(4,128)(2,1)S(1)} async-done(((bf16[4,32,4096]{2,0,1:T(4,128)(2,1)}), bf16[4,32,4096]{2,0,1:T(4,128)(2,1)S(1)}, u32[]{:S(2)}, u32[]{:S(2)}) %all-to-all-start.1) | async-done | bytes 1048608 | tf_op jit(solution)/shard_map/all_to_all | solution.py:23
  71.4 2.1 copy.39
  73.5 2.7 gather_fusion
  76.2 3.9 gather_fusion.1
  80.1 2.9 broadcast_select_fusion.1
  84.0 1.2 fusion.19
  85.3 1.2 fusion.21
  86.6 45.4 %all_gather.14 = bf16[64,1,4096]{2,1,0:T(2,128)(2,1)S(1)} all-gather(bf16[4,1,4096]{2,1,0:T(2,128)(2,1)S(1)} %reshape.215), channel_id=1, replica_groups=mesh['dp'=32,'group'=16] {'group'}, dimensions={0}, use_global_device_ids=true | all-gather | bytes 557056 | tf_op jit(solution)/shard_map/all_gather | solution.py:39
  132.0 2.3 convolution_bitcast_fusion.1
  134.3 37.7 %all_gather.12 = bf16[64,1,4096]{2,1,0:T(2,128)(2,1)S(1)} all-gather(bf16[4,1,4096]{2,1,0:T(2,128)(2,1)S(1)} %reshape.214), channel_id=1, replica_groups=mesh['dp'=32,'group'=16] {'group'}, dimensions={0}, use_global_device_ids=true | all-gather | bytes 557056 | tf_op jit(solution)/shard_map/all_gather | solution.py:40
  172.1 26.4 %all-gather.3.cloned.1.call-done = bf16[1,128,4096]{2,1,0:T(8,128)(2,1)} async-done(((bf16[1,128,128]{2,1,0:T(8,128)(2,1)}), bf16[1,128,4096]{2,1,0:T(8,128)(2,1)}) %all-gather.3.cloned.1.call-update) | async-done | bytes 1048592 | tf_op jit(solution)/shard_map/all_gather | solution.py:44
  198.4 2.4 fusion.5
  200.8 2.0 fusion.9
  202.9 1.3 fusion.4
  204.3 1.3 dynamic-slice
  207.0 156.7 %all-reduce.5.cloned.1.call-done = (bf16[64,1,4096]{2,0,1:T(8,128)(2,1)}, bf16[64,1,4096]{2,0,1:T(8,128)(2,1)}) async-done(((bf16[64,1,4096]{2,0,1:T(8,128)(2,1)}, bf16[64,1,4096]{2,0,1:T(8,128)(2,1)}), (bf16[64,1,4096]{2,0,1:T(8,128)(2,1)}, bf16[64,1,4096]{2,0,1:T(8,128)(2,1)})) %all-reduce.5.cloned.1.call-update) | async-done | bytes 1048592
  366.6 2.1 copy.45
  368.7 3.9 gather_fusion.2
  372.6 2.0 broadcast_select_fusion
  374.6 6.3 all-to-all-start.2
  380.9 1.9 fusion.3
  382.8 5.0 copy.67
  389.0 3.1 fusion.2
  392.9 117.2 %psum.7 = f32[4096,1]{0,1:T(1,128)} all-reduce(f32[4096,1]{0,1:T(1,128)S(1)} %convolution_bitcast_fusion), channel_id=1, replica_groups=mesh['dp'=32,'group'=16] {'dp','group'}, use_global_device_ids=true, to_apply=%region_8.10 | all-reduce | flops 4096 | bytes 32768 | tf_op jit(solution)/shard_map/psum | solution.py:82
  512.2 2.1 copy.46
  514.3 1.6 copy.47
  515.9 107.3 %reduce-scatter.7.cloned.1.call-done = bf16[1,128,128]{2,1,0:T(8,128)(2,1)} async-done(((bf16[1,4096,128]{2,1,0:T(8,128)(2,1)}), bf16[1,128,128]{2,1,0:T(8,128)(2,1)}) %reduce-scatter.7.cloned.1.call-update) | async-done | bytes 32784 | tf_op jit(solution)/shard_map/reduce_scatter | solution.py:58
  (62 shorter events, 11.8 us)
Async XLA Ops:
  7.2 12.3 %copy-start.4 = (bf16[4,32,4096]{2,1,0:T(8,128)(2,1)S(1)}, bf16[4,32,4096]{2,1,0:T(8,128)(2,1)}, u32[]{:S(2)}) copy-start(bf16[4,32,4096]{2,1,0:T(8,128)(2,1)} %param.9) | copy-start | bytes 3145732
  10.3 31.3 %all-to-all-start = ((bf16[4,32,4096]{2,0,1:T(4,128)(2,1)}), bf16[4,32,4096]{2,0,1:T(4,128)(2,1)S(1)}, u32[]{:S(2)}, u32[]{:S(2)}) async-start(bf16[4,32,4096]{2,0,1:T(4,128)(2,1)} %copy.36), calls=%async_computation | async-start | bytes 2097152 | tf_op jit(solution)/shard_map/all_to_all | solution.py:22
  19.5 31.6 %copy-start.6 = (s32[1,64]{1,0:T(1,128)S(1)}, s32[1,64]{1,0:T(1,128)}, u32[]{:S(2)}) copy-start(s32[1,64]{1,0:T(1,128)} %param.10) | copy-start | bytes 772
  41.5 29.9 %all-to-all-start.1 = ((bf16[4,32,4096]{2,0,1:T(4,128)(2,1)}), bf16[4,32,4096]{2,0,1:T(4,128)(2,1)S(1)}, u32[]{:S(2)}, u32[]{:S(2)}) async-start(bf16[4,32,4096]{2,0,1:T(4,128)(2,1)} %copy.38), calls=%async_computation.1 | async-start | bytes 2097152 | tf_op jit(solution)/shard_map/all_to_all | solution.py:23
  49.3 82.7 %all-gather.5.cloned.1.call-start = ((), (), s32[]{:S(2)}) async-start(), calls=%async_computation.6 | async-start | bytes 1081344 | tf_op jit(solution)/shard_map/all_gather | solution.py:43
  50.0 148.4 %all-gather.3.cloned.1.call-start = ((), (), s32[]{:S(2)}) async-start(), calls=%async_computation.5 | async-start | bytes 1081344 | tf_op jit(solution)/shard_map/all_gather | solution.py:44
  50.8 312.9 %all-reduce.5.cloned.1.call-start = ((), (), s32[]{:S(2)}) async-start(), calls=%async_computation.9 | async-start | bytes 2097152
  80.1 2.9 copy-start.5
  83.0 2.3 copy-start.1
  132.0 68.8 %copy-start = (bf16[64,1,4096]{2,1,0:T(2,128)(2,1)}, bf16[64,1,4096]{2,1,0:T(2,128)(2,1)S(1)}, u32[]{:S(2)}) copy-start(bf16[64,1,4096]{2,1,0:T(2,128)(2,1)S(1)} %all_gather.14) | copy-start | bytes 1572868
  198.4 4.4 copy-start.3
  202.9 162.5 %copy-start.2 = (bf16[64,2,4096]{2,1,0:T(2,128)(2,1)S(1)}, bf16[64,2,4096]{2,1,0:T(2,128)(2,1)}, u32[]{:S(2)}) copy-start(bf16[64,2,4096]{2,1,0:T(2,128)(2,1)} %get-tuple-element.23) | copy-start | bytes 3145732
  374.6 137.6 %all-to-all-start.2 = ((bf16[64,2,4096]{2,1,0:T(2,128)(2,1)}), bf16[64,2,4096]{2,1,0:T(2,128)(2,1)}, u32[]{:S(2)}, u32[]{:S(2)}) async-start(bf16[64,2,4096]{2,1,0:T(2,128)(2,1)} %broadcast_select_fusion), calls=%async_computation.2 | async-start | bytes 2097152 | tf_op jit(solution)/shard_map/all_to_all | solution.py:81
  380.9 129.8 %reduce-scatter.9.cloned.1.call-start = ((), (), s32[]{:S(2)}) async-start(), calls=%async_computation.8 | async-start | bytes 1081344
  389.0 234.2 %reduce-scatter.7.cloned.1.call-start = ((), (), s32[]{:S(2)}) async-start(), calls=%async_computation.7 | async-start | bytes 1081344 | tf_op jit(solution)/shard_map/reduce_scatter | solution.py:58
Sparse Core Ops, SparseCore 0:
  53.3 76.4 all-gather.4
  132.8 65.5 all-gather.2
  204.3 159.3 all-reduce.4
  389.1 121.5 reduce-scatter.8
  515.5 107.6 reduce-scatter.6
where the time goes:
time: 632 us; the launch traced here: 630 us
  waiting for transfers between devices  332 us (53%)
  blocking collectives  200 us (32%)
  local copies, waits for them, and re-layouts  35.1 us (6%)
  starting transfers between devices  23.6 us (4%)
  matrix products  18.3 us (3%)
  between operations  14.7 us (2%)
    unnamed x7, waiting for transfers between devices  159 us
    psum x1, blocking collectives, shards(): grad_router = lax.psum(d_route, ('dp', 'group'))  117 us
    reduce_scatter x1, waiting for transfers between devices, shards(): lax.psum_scatter(part_in.astype(jnp.bfloat16), 'dp', scatter_dimension=1,...  107 us
    all_gather x1, blocking collectives, shards(): lax.all_gather(mixed.reshape(local_rows, experts, width), 'group', axis=0...  45.4 us
    all_gather x1, blocking collectives, shards(): lax.all_gather(dmix_out.reshape(local_rows, experts, width), 'group', axi...  37.7 us
    all_gather x1, waiting for transfers between devices, shards(): lax.all_gather(w_out, 'dp', axis=2, tiled=True)  26.4 us
    all_to_all x1, waiting for transfers between devices, shards(): lax.all_to_all(tokens, 'group', split_axis=1, concat_axis=0, tiled=True)  20.3 us
    all_to_all x1, waiting for transfers between devices, shards(): lax.all_to_all(grad_out, 'group', split_axis=1, concat_axis=0, tiled=True)  19.2 us
  transfers between devices with their start and end apart: 8, of which 6 were waited for; matrix products, arithmetic and copies ran while one was open for 6% of the time, Pallas kernels for 0%

commit v1 on v0

v1 whole, which is shorter than its diff:
```python
import jax
import jax.numpy as jnp
from jax import lax
from jax.experimental import pallas as pl
from jax.experimental.pallas import tpu as pltpu
from jax.sharding import Mesh, PartitionSpec as P

BF = jnp.bfloat16
F32 = jnp.float32
LOWEST = -1e30
NX, NH, NC, NL, NY = 4, 4, 2, 4, 4
AXES = ("x", "zh", "core", "zl", "y")
HERE, THERE = 32, 32
LIMIT = 32 * 1024 * 1024


def call(body, outs, vmem_args, smem_args=(), flops=0):
    multi = isinstance(outs, (list, tuple))
    arrays = list(smem_args) + list(vmem_args)
    nbytes = sum(a.size * a.dtype.itemsize for a in arrays)
    for o in outs if multi else [outs]:
        nbytes += o.size * o.dtype.itemsize
    vm = pl.BlockSpec(memory_space=pltpu.VMEM)
    sm = pl.BlockSpec(memory_space=pltpu.SMEM)
    return pl.pallas_call(
        body,
        out_shape=outs,
        in_specs=[sm] * len(smem_args) + [vm] * len(vmem_args),
        out_specs=[vm] * len(outs) if multi else vm,
        compiler_params=pltpu.CompilerParams(vmem_limit_bytes=LIMIT),
        cost_estimate=pl.CostEstimate(flops=flops, bytes_accessed=nbytes, transcendentals=0),
    )(*arrays)


def sds(shape, dtype=BF):
    return jax.ShapeDtypeStruct(shape, dtype)


def three(value):
    a = value.astype(BF).astype(F32)
    b = (value - a).astype(BF).astype(F32)
    c = (value - a - b).astype(BF).astype(F32)
    return a, b, c


def pack_stats(top, total):
    lane = lax.broadcasted_iota(jnp.int32, (top.shape[0], 128), 1)
    out = jnp.zeros((top.shape[0], 128), F32)
    for i, term in enumerate(three(top) + three(total)):
        out = jnp.where(lane == i, term, out)
    return out.astype(BF)


def unpack_stats(packed):
    packed = packed.astype(F32)
    lanes = [packed[:, i : i + 1] for i in range(6)]
    return (lanes[0] + lanes[1]) + lanes[2], (lanes[3] + lanes[4]) + lanes[5]


def merge_stats(stats):
    top = stats[0][0]
    for m, _ in stats[1:]:
        top = jnp.maximum(top, m)
    factors = [jnp.exp(m - top) for m, _ in stats]
    total = factors[0] * stats[0][1]
    for f, (_, s) in zip(factors[1:], stats[1:]):
        total = total + f * s
    return top, factors, total


def partial_body(kind, tok, grd, route, out, logit):
    ls = []
    for s in range(4):
        acc = jnp.zeros((32, 512), F32)
        for j in range(8):
            d = slice(j * 512, j * 512 + 512)
            acc = acc + tok[s, :, d].astype(F32) * route[:, d].astype(F32)
        l = jnp.sum(acc, axis=1, keepdims=True)
        ls.append(l)
        logit[s] = jnp.broadcast_to(l, (32, 128))
    tops, sums, weights = [], [], []
    for k in range(2):
        top = jnp.full((32, 1), LOWEST, F32)
        for s in range(4):
            top = jnp.maximum(top, jnp.where(kind[s] == k, ls[s], LOWEST))
        ws = [jnp.where(kind[s] == k, jnp.exp(jnp.minimum(ls[s] - top, 0.0)), 0.0) for s in range(4)]
        tops.append(top)
        sums.append((ws[0] + ws[1]) + (ws[2] + ws[3]))
        weights.append(ws)
    stats = pack_stats(jnp.concatenate(tops, 0), jnp.concatenate(sums, 0))
    for y in range(NY):
        for j in range(4):
            out[y, 128:144, j * 128 : j * 128 + 128] = stats[j * 16 : j * 16 + 16]
        out[y, 128:144, 512:1024] = jnp.zeros((16, 512), BF)
        for h in range(4):
            d = slice(y * 1024 + h * 256, y * 1024 + h * 256 + 256)
            o = slice(h * 256, h * 256 + 256)
            for base, ref in ((0, tok), (64, grd)):
                vals = [ref[s, :, d].astype(F32) for s in range(4)]
                for k in range(2):
                    w = weights[k]
                    acc = (w[0] * vals[0] + w[1] * vals[1]) + (w[2] * vals[2] + w[3] * vals[3])
                    out[y, base + k * 32 : base + k * 32 + 32, o] = acc.astype(BF)


def over_y_body(got, out):
    stats = []
    for i in range(NY):
        rows = [got[i, 128:144, j * 128 : j * 128 + 128] for j in range(4)]
        stats.append(unpack_stats(jnp.concatenate(rows, 0)))
    top, factors, total = merge_stats(stats)
    packed = pack_stats(top, total)
    for z in range(NL):
        for j in range(2):
            out[z, 128:160, j * 128 : j * 128 + 128] = packed[j * 32 : j * 32 + 32]
        for base in (0, 64):
            acc = factors[0] * got[0, base : base + 64, z * 256 : z * 256 + 256].astype(F32)
            for i in range(1, NY):
                acc = acc + factors[i] * got[i, base : base + 64, z * 256 : z * 256 + 256].astype(F32)
            out[z, base : base + 64, :] = acc.astype(BF)


def over_zl_body(got, out, final):
    stats = []
    for i in range(NL):
        rows = [got[i, 128:160, j * 128 : j * 128 + 128] for j in range(2)]
        stats.append(unpack_stats(jnp.concatenate(rows, 0)))
    top, factors, total = merge_stats(stats)
    scale = 1.0 / total
    lane = lax.broadcasted_iota(jnp.int32, (64, 128), 1)
    final[...] = jnp.where(lane == 0, top, total)
    factors = [f * scale for f in factors]
    for base in (0, 64):
        acc = factors[0] * got[0, base : base + 64].astype(F32)
        for i in range(1, NL):
            acc = acc + factors[i] * got[i, base : base + 64].astype(F32)
        acc = acc.astype(BF)
        for z in range(NL):
            out[z, base : base + 64] = acc


def weight_blocks(core, own, other, h, c):
    mine = core == c
    ins = [jnp.where(mine, own[a, h, :128], other[a, h, :128]) for a in range(NX)]
    outs = [jnp.where(mine, own[a, h, 128:], other[a, h, 128:]) for a in range(NX)]
    return jnp.concatenate(ins, 1), jnp.concatenate(outs, 0)


def hidden_body(core, mixed, own, other, out):
    hid = jnp.zeros((64, 512), F32)
    dact = jnp.zeros((64, 512), F32)
    for h in range(NH):
        for c in range(NC):
            win, wout = weight_blocks(core[0], own, other, h, c)
            lanes = slice(c * 128, c * 128 + 128)
            hid = hid + jnp.dot(mixed[h, :64, lanes], win, preferred_element_type=F32)
            dact = dact + lax.dot_general(
                mixed[h, 64:, lanes], wout, (((1,), (1,)), ((), ())), preferred_element_type=F32
            )
    hid = hid.astype(BF)
    dact = dact.astype(BF)
    for y in range(NY):
        out[y, :64] = hid
        out[y, 64:] = dact


def expert_body(core, got, own, other, out, inner):
    hid = got[0, :64].astype(F32)
    dact = got[0, 64:].astype(F32)
    for i in range(1, NY):
        hid = hid + got[i, :64].astype(F32)
        dact = dact + got[i, 64:].astype(F32)
    sigma = jax.nn.sigmoid(hid)
    act = (hid * sigma).astype(BF)
    dpre = (dact * (sigma * (1.0 + hid * (1.0 - sigma)))).astype(BF)
    inner[:64] = act
    inner[64:] = dpre
    for h in range(NH):
        for c in range(NC):
            win, wout = weight_blocks(core[0], own, other, h, c)
            lanes = slice(c * 128, c * 128 + 128)
            out[h, :64, lanes] = jnp.dot(act, wout, preferred_element_type=F32).astype(BF)
            out[h, 64:, lanes] = lax.dot_general(
                dpre, win, (((1,), (1,)), ((), ())), preferred_element_type=F32
            ).astype(BF)


def weight_grad_body(mixed, mixed_other, inner, inner_other, out):
    act = jnp.concatenate([inner[:64], inner_other[:64]], 0)
    dpre = jnp.concatenate([inner[64:], inner_other[64:]], 0)
    for h in range(NH):
        mix = jnp.concatenate([mixed[h, :64], mixed_other[h, :64]], 0)
        dmo = jnp.concatenate([mixed[h, 64:], mixed_other[h, 64:]], 0)
        gin = lax.dot_general(mix, dpre, (((0,), (0,)), ((), ())), preferred_element_type=F32)
        gout = lax.dot_general(act, dmo, (((0,), (0,)), ((), ())), preferred_element_type=F32)
        for a in range(NX):
            out[a, h, :128] = gin[:, a * 128 : a * 128 + 128].astype(BF)
            out[a, h, 128:] = gout[a * 128 : a * 128 + 128].astype(BF)


def sum_four_body(got, out):
    acc = got[0].astype(F32)
    for i in range(1, NL):
        acc = acc + got[i].astype(F32)
    acc = acc.astype(BF)
    for z in range(NL):
        out[z] = acc


def mix_of(kind, logit, final, s):
    rows = pl.ds(pl.multiple_of(kind[s] * 32, 32), 32)
    return jnp.exp(logit[s][:, 0:1] - final[rows, 0:1]) / final[rows, 1:2]


def slope_body(kind, tok, grd, back, logit, final, out, dmix):
    centres = [jnp.zeros((32, 1), F32), jnp.zeros((32, 1), F32)]
    for s in range(4):
        top = pl.multiple_of(kind[s] * 32, 32)
        acc = jnp.zeros((32, 256), F32)
        for y in range(NY):
            for z in range(NL):
                d = slice(y * 1024 + z * 256, y * 1024 + z * 256 + 256)
                eo = back[y, z, pl.ds(top, 32), :].astype(F32)
                dm = back[y, z, pl.ds(top + 64, 32), :].astype(F32)
                acc = acc + (grd[s, :, d].astype(F32) * eo + tok[s, :, d].astype(F32) * dm)
        dm = jnp.sum(acc, axis=1, keepdims=True)
        dmix[s] = jnp.broadcast_to(dm, (32, 128))
        term = mix_of(kind, logit, final, s) * dm
        for k in range(2):
            centres[k] = centres[k] + jnp.where(kind[s] == k, term, 0.0)
    lane = lax.broadcasted_iota(jnp.int32, (8, 128), 1)
    tile = jnp.zeros((8, 128), F32)
    for k in range(2):
        for j in range(4):
            tile = jnp.where(lane == k * 4 + j, centres[k][j * 8 : j * 8 + 8], tile)
    for g in range(NL * NY):
        out[g] = tile


def final_body(kind, tok, back, logit, final, dmix, got, route, dtok, droute):
    tile = got[0]
    for g in range(1, NL * NY):
        tile = tile + got[g]
    centres = [
        jnp.concatenate([tile[:, k * 4 + j : k * 4 + j + 1] for j in range(4)], 0) for k in range(2)
    ]
    mixb, dlogit, tops = [], [], []
    for s in range(4):
        mix = mix_of(kind, logit, final, s)
        centre = jnp.where(kind[s] == 0, centres[0], centres[1])
        dlogit.append((mix * (dmix[s][:, 0:1] - centre)).astype(BF).astype(F32))
        mixb.append(mix.astype(BF).astype(F32))
        tops.append(pl.multiple_of(kind[s] * 32 + 64, 32))
    for y in range(NY):
        for z in range(NL):
            d = slice(y * 1024 + z * 256, y * 1024 + z * 256 + 256)
            r = route[:, d].astype(F32)
            acc = jnp.zeros((32, 256), F32)
            for s in range(4):
                dm = back[y, z, pl.ds(tops[s], 32), :].astype(F32)
                dtok[s, :, d] = (mixb[s] * dm + dlogit[s] * r).astype(BF)
                acc = acc + tok[s, :, d].astype(F32) * dlogit[s]
            total = jnp.sum(acc, axis=0, keepdims=True)
            i = (y * NL + z) // 2
            o = slice((z % 2) * 256, (z % 2) * 256 + 256)
            for g in range(16):
                droute[g, i : i + 1, o] = total


def shards(tokens, grad_out, members, router, w_in, w_out):
    def swap(value, axes):
        return lax.all_to_all(value, axes, split_axis=0, concat_axis=0, tiled=True)

    core = lax.axis_index("core")
    core_s = jnp.full((1,), core, jnp.int32)
    group = lax.axis_index(("zl", "y"))
    flip = [(a * 4 + b, b * 4 + a) for a in range(4) for b in range(4)]
    cores = [(0, 1), (1, 0)]

    shard = jnp.concatenate([w_in[0], w_out[0]], axis=0)
    shard = lax.ppermute(shard, ("x", "y"), flip)
    shard = lax.all_gather(shard, "zh", axis=0, tiled=False)
    shard = swap(jnp.broadcast_to(shard[None], (NX, NH, 256, 128)), "x")
    other = lax.ppermute(shard, "core", cores)

    mine = group * 4 + jnp.arange(4, dtype=jnp.int32)
    kind = jnp.any(members[0, 32:][None, :] == mine[:, None], axis=1).astype(jnp.int32)
    route = router.reshape(1, 4096)

    sent, logit = call(
        partial_body,
        [sds((NY, 144, 1024)), sds((4, 32, 128), F32)],
        (tokens, grad_out, route),
        (kind,),
        flops=10_000_000,
    )
    sent = call(over_y_body, sds((NL, 160, 256)), (swap(sent, "y"),), flops=1_000_000)
    sent, final = call(
        over_zl_body, [sds((NL, 128, 256)), sds((64, 128), F32)], (swap(sent, "zl"),), flops=300_000
    )
    mixed = swap(sent, "zl")
    half = lax.dynamic_slice_in_dim(mixed, (1 - core) * 128, 128, axis=2)
    mixed_half = lax.dynamic_slice_in_dim(mixed, core * 128, 128, axis=2)
    mixed_other = lax.ppermute(half, "core", cores)

    sent = call(hidden_body, sds((NY, 128, 512)), (mixed, shard, other), (core_s,), flops=140_000_000)
    sent, inner = call(
        expert_body,
        [sds((NL, 128, 256)), sds((128, 512))],
        (swap(sent, "y"), shard, other),
        (core_s,),
        flops=140_000_000,
    )
    inner_other = lax.ppermute(inner, "core", cores)
    grads = call(
        weight_grad_body,
        sds((NX, NH, 256, 128)),
        (mixed_half, mixed_other, inner, inner_other),
        flops=140_000_000,
    )
    grads = lax.psum_scatter(grads.reshape(NX * NH * 256, 128), "x", scatter_dimension=0, tiled=True)
    grads = lax.psum_scatter(grads, "zh", scatter_dimension=0, tiled=True)
    grads = lax.ppermute(grads, ("x", "y"), flip)

    sent = call(sum_four_body, sds((NL, 128, 256)), (swap(sent, "zl"),), flops=300_000)
    sent = swap(sent, "zl")
    back = swap(jnp.broadcast_to(sent[None], (NY, NL, 128, 256)), "y")
    sent, dmix = call(
        slope_body,
        [sds((16, 8, 128), F32), sds((4, 32, 128), F32)],
        (tokens, grad_out, back, logit, final),
        (kind,),
        flops=5_000_000,
    )
    grad_tokens, droute = call(
        final_body,
        [sds((4, 32, 4096)), sds((16, 8, 512), F32)],
        (tokens, back, logit, final, dmix, swap(sent, ("zl", "y")), route),
        (kind,),
        flops=5_000_000,
    )
    droute = jnp.sum(swap(droute, ("x", "y")), axis=0)
    droute = jnp.sum(swap(jnp.broadcast_to(droute[None], (16, 8, 512)), ("zh", "zl")), axis=0)
    droute = droute + lax.ppermute(droute, "core", cores)
    return grad_tokens, grads[None, :128], grads[None, 128:], droute.reshape(4096, 1)


def solution(mesh):
    fine = Mesh(mesh.devices.reshape(NX, NH, NC, NL, NY), AXES)
    dp, group = ("x", "zh", "core"), ("zl", "y")
    return jax.shard_map(
        shards,
        mesh=fine,
        in_specs=(
            P(dp + group, None, None),
            P(dp + group, None, None),
            P(dp, None),
            P(),
            P(None, dp, group),
            P(None, group, dp),
        ),
        out_specs=(P(dp + group, None, None), P(None, dp, group), P(None, group, dp), P()),
        check_vma=False,
    )
```

time: 632 us -> 244 us (0.39)
  the two profiles are of different devices: /device:TPU:1 before, /device:TPU:4 now
where the time goes in v1:
time: 244 us; the launch traced here: 243 us
  blocking collectives  91.2 us (37%)
  waiting for transfers between devices  66.9 us (27%)
  starting transfers between devices  50.9 us (21%)
  between operations  14.2 us (6%)
  Pallas kernels  12.3 us (5%)
  local copies, waits for them, and re-layouts  7.21 us (3%)
    all_to_all x5, blocking collectives, swap(): return lax.all_to_all(value, axes, split_axis=0, concat_axis=0, tiled=True)  66.5 us
    reduce_scatter x1, waiting for transfers between devices, shards(): grads = lax.psum_scatter(grads, 'zh', scatter_dimension=0, tiled=True)  40.2 us
    all_to_all x6, starting transfers between devices, swap(): return lax.all_to_all(value, axes, split_axis=0, concat_axis=0, tiled=True)  27.9 us
    all_gather x1, blocking collectives, shards(): shard = lax.all_gather(shard, 'zh', axis=0, tiled=False)  24.7 us
    all_to_all x6, waiting for transfers between devices, swap(): return lax.all_to_all(value, axes, split_axis=0, concat_axis=0, tiled=True)  19.3 us
    pallas_call x9, Pallas kernels, call(): pl.pallas_call(body, out_shape=outs, in_specs=[sm] * len(smem_args) + [vm...  12.3 us
    ppermute x1, starting transfers between devices, shards(): shard = lax.ppermute(shard, ('x', 'y'), flip)  9.79 us
    ppermute x1, starting transfers between devices, shards(): grads = lax.ppermute(grads, ('x', 'y'), flip)  4.9 us
  transfers between devices with their start and end apart: 14, of which 7 were waited for; matrix products, arithmetic and copies ran while one was open for 1% of the time, Pallas kernels for 3%

profile of v1, /device:TPU:4, one launch (start us, length us, event | category | flops | bytes accessed | tf_op | source)
XLA Modules:
  0.0 243.0 jit_solution(1402513916834305761)
XLA Ops:
  8.1 1.2 copy-done
  9.3 1.2 copy-done.2
  11.3 2.8 %shard_map.93 = (bf16[4,144,1024]{2,1,0:T(8,128)(2,1)}, f32[4,32,128]{2,1,0:T(8,128)S(1)}) custom-call(s32[4]{0:T(128)S(1)} %convert_element_type.3.kind, bf16[4,32,4096]{2,1,0:T(8,128)(2,1)S(1)} %copy-done, bf16[4,32,4096]{2,1,0:T(8,128)(2,1)S(1)} %copy-done.2, bf16[1,4096]{1,0:T(2,128)(2,1)S(1)} %bitcast.17), custom_call_target="tpu_custom_call" | custom-call | flops 10000000 | bytes 3350544 | tf_op jit(solution)/shard_map/pallas_call | solution.py:25
  14.0 4.6 %all-to-all-start = ((bf16[4,144,1024]{2,1,0:T(8,128)(2,1)}), bf16[4,144,1024]{2,1,0:T(8,128)(2,1)S(1)}, u32[]{:S(2)}, u32[]{:S(2)}) async-start(bf16[4,144,1024]{2,1,0:T(8,128)(2,1)} %get-tuple-element.14), calls=%async_computation | async-start | bytes 2359296 | tf_op jit(solution)/shard_map/all_to_all | solution.py:272
  18.7 9.8 %collective-permute-start = (bf16[256,128]{1,0:T(8,128)(2,1)S(1)}, bf16[256,128]{1,0:T(8,128)(2,1)S(1)}, u32[]{:S(2)}, u32[]{:S(2)}) collective-permute-start(bf16[256,128]{1,0:T(8,128)(2,1)S(1)} %pad_maximum_fusion), channel_id=1, source_target_pairs={{0,0},{1,128},{2,256},{3,384},{128,1},{129,129},{130,257},{131,385... | collective-permute-start | bytes 196616 | tf_op jit(solution)/shard_map/ppermute | solution.py:281
  28.4 2.3 collective-permute-done
  30.8 24.7 %all-gather = bf16[1024,128]{1,0:T(8,128)(2,1)S(1)} all-gather(bf16[256,128]{1,0:T(8,128)(2,1)S(1)} %collective-permute-done), channel_id=2, replica_groups=mesh['x'=4,'zh'=4,'core'=2,'zl'=4,'y'=4] {'zh'}, dimensions={0}, use_global_device_ids=true | all-gather | bytes 327680 | tf_op jit(solution)/shard_map/all_gather | solution.py:282
  55.5 1.2 broadcast_in_dim.13
  56.6 6.1 %all-to-all-start.3 = ((bf16[4,4,256,128]{3,2,1,0:T(8,128)(2,1)}), bf16[4,4,256,128]{3,2,1,0:T(8,128)(2,1)S(1)}, u32[]{:S(2)}, u32[]{:S(2)}) async-start(bf16[4,4,256,128]{3,2,1,0:T(8,128)(2,1)} %broadcast_in_dim.13), calls=%async_computation.3 | async-start | bytes 2097152 | tf_op jit(solution)/shard_map/all_to_all | solution.py:272
  62.8 1.1 shard_map.94
  63.9 7.2 %all-to-all-done.3.own = bf16[4,4,256,128]{3,2,1,0:T(8,128)(2,1)S(1)} async-done(((bf16[4,4,256,128]{3,2,1,0:T(8,128)(2,1)}), bf16[4,4,256,128]{3,2,1,0:T(8,128)(2,1)S(1)}, u32[]{:S(2)}, u32[]{:S(2)}) %all-to-all-start.3) | async-done | bytes 1048608 | tf_op jit(solution)/shard_map/all_to_all | solution.py:272
  71.1 3.5 %all-to-all-start.1 = ((bf16[4,160,256]{2,1,0:T(8,128)(2,1)}), bf16[4,160,256]{2,1,0:T(8,128)(2,1)S(1)}, u32[]{:S(2)}, u32[]{:S(2)}) async-start(bf16[4,160,256]{2,1,0:T(8,128)(2,1)} %shard_map.94), calls=%async_computation.1 | async-start | bytes 655360 | tf_op jit(solution)/shard_map/all_to_all | solution.py:272
  74.6 1.9 collective-permute-start.1
  76.5 5.3 %all-to-all-done.1.got = bf16[4,160,256]{2,1,0:T(8,128)(2,1)S(1)} async-done(((bf16[4,160,256]{2,1,0:T(8,128)(2,1)}), bf16[4,160,256]{2,1,0:T(8,128)(2,1)S(1)}, u32[]{:S(2)}, u32[]{:S(2)}) %all-to-all-start.1) | async-done | bytes 327712 | tf_op jit(solution)/shard_map/all_to_all | solution.py:272
  82.8 3.6 %all-to-all-start.2 = ((bf16[4,128,256]{2,1,0:T(8,128)(2,1)}), bf16[4,128,256]{2,1,0:T(8,128)(2,1)S(1)}, u32[]{:S(2)}, u32[]{:S(2)}) async-start(bf16[4,128,256]{2,1,0:T(8,128)(2,1)} %get-tuple-element.15), calls=%async_computation.2 | async-start | bytes 524288 | tf_op jit(solution)/shard_map/all_to_all | solution.py:272
  86.5 6.8 %all-to-all-done.2.mixed = bf16[4,128,256]{2,1,0:T(8,128)(2,1)S(1)} async-done(((bf16[4,128,256]{2,1,0:T(8,128)(2,1)}), bf16[4,128,256]{2,1,0:T(8,128)(2,1)S(1)}, u32[]{:S(2)}, u32[]{:S(2)}) %all-to-all-start.2) | async-done | bytes 262176 | tf_op jit(solution)/shard_map/all_to_all | solution.py:272
  94.0 11.7 %all_to_all.55.got = bf16[4,128,512]{2,1,0:T(8,128)(2,1)S(1)} all-to-all(bf16[4,128,512]{2,1,0:T(8,128)(2,1)S(1)} %shard_map.96), channel_id=1, replica_groups=mesh['x'=4,'zh'=4,'core'=2,'zl'=4,'y'=4] {'y'}, dimensions={0} | all-to-all | bytes 1048576 | tf_op jit(solution)/shard_map/all_to_all | solution.py:272
  106.4 10.5 %all_to_all.56.got = bf16[4,128,256]{2,1,0:T(8,128)(2,1)S(1)} all-to-all(bf16[4,128,256]{2,1,0:T(8,128)(2,1)S(1)} %get-tuple-element.16), channel_id=1, replica_groups=mesh['x'=4,'zh'=4,'core'=2,'zl'=4,'y'=4] {'zl'}, dimensions={0} | all-to-all | bytes 524288 | tf_op jit(solution)/shard_map/all_to_all | solution.py:272
  117.6 3.4 %all-to-all-start.6 = ((bf16[4,128,256]{2,1,0:T(8,128)(2,1)}), bf16[4,128,256]{2,1,0:T(8,128)(2,1)S(1)}, u32[]{:S(2)}, u32[]{:S(2)}) async-start(bf16[4,128,256]{2,1,0:T(8,128)(2,1)} %shard_map.98), calls=%async_computation.6 | async-start | bytes 524288 | tf_op jit(solution)/shard_map/all_to_all | solution.py:272
  121.2 1.9 collective-permute-start.2
  123.1 2.4 collective-permute-start.3
  126.5 1.5 shard_map.101
  128.1 18.5 %all_to_all.57.back = bf16[4,4,128,256]{3,2,1,0:T(8,128)(2,1)S(1)} all-to-all(bf16[4,4,128,256]{3,2,1,0:T(8,128)(2,1)S(1)} %broadcast_in_dim.14), channel_id=1, replica_groups=mesh['x'=4,'zh'=4,'core'=2,'zl'=4,'y'=4] {'y'}, dimensions={0} | all-to-all | bytes 2097152 | tf_op jit(solution)/shard_map/all_to_all | solution.py:272
  146.6 1.2 shard_map.99
  147.8 13.9 %all_to_all.58.got = f32[16,8,128]{2,1,0:T(8,128)S(1)} all-to-all(f32[16,8,128]{2,1,0:T(8,128)S(1)} %get-tuple-element.20), channel_id=1, replica_groups=mesh['x'=4,'zh'=4,'core'=2,'zl'=4,'y'=4] {'zl','y'}, dimensions={0} | all-to-all | bytes 131072 | tf_op jit(solution)/shard_map/all_to_all | solution.py:272
  161.7 2.5 %shard_map.100 = (bf16[4,32,4096]{2,1,0:T(8,128)(2,1)}, f32[16,8,512]{2,1,0:T(8,128)S(1)}) custom-call(s32[4]{0:T(128)S(1)} %convert_element_type.3.kind, bf16[4,32,4096]{2,1,0:T(8,128)(2,1)S(1)} %copy-done.1, bf16[4,4,128,256]{3,2,1,0:T(8,128)(2,1)S(1)} %all_to_all.57.back, f32[4,32,128]{2,1,0:T(8,128)S(1)} %get-tuple-element.17.logit, ...), custom_call_target="tpu_custom_call" | custom-call | flops 5000000 | bytes 3645456 | tf_op jit(solution)/shard_map/pallas_call | solution.py:25
  164.2 12.0 %all_to_all.59 = f32[16,8,512]{2,1,0:T(8,128)S(1)} all-to-all(f32[16,8,512]{2,1,0:T(8,128)S(1)} %get-tuple-element.23), channel_id=1, replica_groups=mesh['x'=4,'zh'=4,'core'=2,'zl'=4,'y'=4] {'x','y'}, dimensions={0} | all-to-all | bytes 524288 | tf_op jit(solution)/shard_map/all_to_all | solution.py:272
  176.9 6.8 %all-to-all-start.10 = ((f32[16,8,512]{2,1,0:T(8,128)}), f32[16,8,512]{2,1,0:T(8,128)S(1)}, u32[]{:S(2)}, u32[]{:S(2)}) async-start(f32[16,8,512]{2,1,0:T(8,128)} %broadcast_in_dim.33), calls=%async_computation.12 | async-start | bytes 524288 | tf_op jit(solution)/shard_map/all_to_all | solution.py:272
  184.5 40.2 %reduce-scatter.5.cloned.1.call-done = bf16[256,128]{1,0:T(8,128)(2,1)} async-done(((bf16[1024,128]{1,0:T(8,128)(2,1)}), bf16[256,128]{1,0:T(8,128)(2,1)}) %reduce-scatter.5.cloned.1.call-update) | async-done | bytes 65552 | tf_op jit(solution)/shard_map/reduce_scatter | solution.py:322
  224.7 4.9 %collective-permute-start.4 = (bf16[256,128]{1,0:T(8,128)(2,1)}, bf16[256,128]{1,0:T(8,128)(2,1)S(1)}, u32[]{:S(2)}, u32[]{:S(2)}) collective-permute-start(bf16[256,128]{1,0:T(8,128)(2,1)} %reduce-scatter.5.cloned.1.call-done), channel_id=1, source_target_pairs={{0,0},{1,128},{2,256},{3,384},{128,1},{129,129},{130,257},{131,385... | collective-permute-start | bytes 196616 | tf_op jit(solution)/shard_map/ppermute | solution.py:323
  229.6 1.9 collective-permute-start.5
  231.5 3.4 %collective-permute-done.4 = bf16[256,128]{1,0:T(8,128)(2,1)S(1)} collective-permute-done((bf16[256,128]{1,0:T(8,128)(2,1)}, bf16[256,128]{1,0:T(8,128)(2,1)S(1)}, u32[]{:S(2)}, u32[]{:S(2)}) %collective-permute-start.4) | collective-permute-done | bytes 65568 | tf_op jit(solution)/shard_map/ppermute | solution.py:323
  (43 shorter events, 8.8 us)
Async XLA Ops:
  8.1 1.2 copy-start
  9.3 1.2 copy-start.2
  10.6 0.7 copy-start.4
  14.0 4.6 %copy-start.6 = (bf16[1,128,128]{2,1,0:T(8,128)(2,1)S(1)}, bf16[1,128,128]{2,1,0:T(8,128)(2,1)}, u32[]{:S(2)}) copy-start(bf16[1,128,128]{2,1,0:T(8,128)(2,1)} %param.11) | copy-start | bytes 98308
  14.0 4.6 %copy-start.7 = (bf16[1,128,128]{2,1,0:T(8,128)(2,1)S(1)}, bf16[1,128,128]{2,1,0:T(8,128)(2,1)}, u32[]{:S(2)}) copy-start(bf16[1,128,128]{2,1,0:T(8,128)(2,1)} %param.10) | copy-start | bytes 98308
  14.0 41.4 %all-to-all-start = ((bf16[4,144,1024]{2,1,0:T(8,128)(2,1)}), bf16[4,144,1024]{2,1,0:T(8,128)(2,1)S(1)}, u32[]{:S(2)}, u32[]{:S(2)}) async-start(bf16[4,144,1024]{2,1,0:T(8,128)(2,1)} %get-tuple-element.14), calls=%async_computation | async-start | bytes 2359296 | tf_op jit(solution)/shard_map/all_to_all | solution.py:272
  18.7 12.1 %collective-permute-start = (bf16[256,128]{1,0:T(8,128)(2,1)S(1)}, bf16[256,128]{1,0:T(8,128)(2,1)S(1)}, u32[]{:S(2)}, u32[]{:S(2)}) collective-permute-start(bf16[256,128]{1,0:T(8,128)(2,1)S(1)} %pad_maximum_fusion), channel_id=1, source_target_pairs={{0,0},{1,128},{2,256},{3,384},{128,1},{129,129},{130,257},{131,385... | collective-permute-start | bytes 196616 | tf_op jit(solution)/shard_map/ppermute | solution.py:281
  56.6 14.5 %all-to-all-start.3 = ((bf16[4,4,256,128]{3,2,1,0:T(8,128)(2,1)}), bf16[4,4,256,128]{3,2,1,0:T(8,128)(2,1)S(1)}, u32[]{:S(2)}, u32[]{:S(2)}) async-start(bf16[4,4,256,128]{3,2,1,0:T(8,128)(2,1)} %broadcast_in_dim.13), calls=%async_computation.3 | async-start | bytes 2097152 | tf_op jit(solution)/shard_map/all_to_all | solution.py:272
  71.1 10.7 %all-to-all-start.1 = ((bf16[4,160,256]{2,1,0:T(8,128)(2,1)}), bf16[4,160,256]{2,1,0:T(8,128)(2,1)S(1)}, u32[]{:S(2)}, u32[]{:S(2)}) async-start(bf16[4,160,256]{2,1,0:T(8,128)(2,1)} %shard_map.94), calls=%async_computation.1 | async-start | bytes 655360 | tf_op jit(solution)/shard_map/all_to_all | solution.py:272
  74.6 11.9 %collective-permute-start.1 = (bf16[4,4,256,128]{3,2,1,0:T(8,128)(2,1)S(1)}, bf16[4,4,256,128]{3,2,1,0:T(8,128)(2,1)S(1)}, u32[]{:S(2)}, u32[]{:S(2)}) collective-permute-start(bf16[4,4,256,128]{3,2,1,0:T(8,128)(2,1)S(1)} %all-to-all-done.3.own), channel_id=1, source_target_pairs={{0,16},{16,0},{1,17},{17,1},{2,18},{18,2},{3,19},{19,3},{4,20},{20... | collective-permute-start | bytes 3145736 | tf_op jit(solution)/shard_map/ppermute | solution.py:284
  82.8 10.4 %all-to-all-start.2 = ((bf16[4,128,256]{2,1,0:T(8,128)(2,1)}), bf16[4,128,256]{2,1,0:T(8,128)(2,1)S(1)}, u32[]{:S(2)}, u32[]{:S(2)}) async-start(bf16[4,128,256]{2,1,0:T(8,128)(2,1)} %get-tuple-element.15), calls=%async_computation.2 | async-start | bytes 524288 | tf_op jit(solution)/shard_map/all_to_all | solution.py:272
  117.6 10.3 %all-to-all-start.6 = ((bf16[4,128,256]{2,1,0:T(8,128)(2,1)}), bf16[4,128,256]{2,1,0:T(8,128)(2,1)S(1)}, u32[]{:S(2)}, u32[]{:S(2)}) async-start(bf16[4,128,256]{2,1,0:T(8,128)(2,1)} %shard_map.98), calls=%async_computation.6 | async-start | bytes 524288 | tf_op jit(solution)/shard_map/all_to_all | solution.py:272
  121.1 62.7 %reduce-scatter.3.cloned.1.call-start = ((), (), s32[]{:S(2)}) async-start(), calls=%async_computation.13 | async-start | bytes 1310720 | tf_op jit(solution)/shard_map/reduce_scatter | solution.py:321
  121.2 4.3 %collective-permute-start.2 = (bf16[4,128,128]{2,1,0:T(8,128)(2,1)S(1)}, bf16[4,128,128]{2,1,0:T(8,128)(2,1)S(1)}, u32[]{:S(2)}, u32[]{:S(2)}) collective-permute-start(bf16[4,128,128]{2,1,0:T(8,128)(2,1)S(1)} %get-tuple-element.24), channel_id=1, source_target_pairs={{0,16},{16,0},{1,17},{17,1},{2,18},{18,2},{3,19},{19,3},{4,20},{20... | collective-permute-start | bytes 393224 | tf_op jit(solution)/shard_map/ppermute | solution.py:304
  123.1 3.4 %collective-permute-start.3 = (bf16[128,512]{1,0:T(8,128)(2,1)S(1)}, bf16[128,512]{1,0:T(8,128)(2,1)S(1)}, u32[]{:S(2)}, u32[]{:S(2)}) collective-permute-start(bf16[128,512]{1,0:T(8,128)(2,1)S(1)} %get-tuple-element.22.inner), channel_id=1, source_target_pairs={{0,16},{16,0},{1,17},{17,1},{2,18},{18,2},{3,19},{19,3},{4,20},{20... | collective-permute-start | bytes 393224 | tf_op jit(solution)/shard_map/ppermute | solution.py:314
  128.1 18.5 %copy-start.1 = (bf16[4,32,4096]{2,1,0:T(8,128)(2,1)S(1)}, bf16[4,32,4096]{2,1,0:T(8,128)(2,1)}, u32[]{:S(2)}) copy-start(bf16[4,32,4096]{2,1,0:T(8,128)(2,1)} %tok.5) | copy-start | bytes 3145732
  128.1 18.5 %copy-start.3 = (bf16[4,32,4096]{2,1,0:T(8,128)(2,1)S(1)}, bf16[4,32,4096]{2,1,0:T(8,128)(2,1)}, u32[]{:S(2)}) copy-start(bf16[4,32,4096]{2,1,0:T(8,128)(2,1)} %grd.3) | copy-start | bytes 3145732
  146.6 15.2 %copy-start.5 = (bf16[4096,1]{0,1:T(2,128)(2,1)S(1)}, bf16[4096,1]{0,1:T(2,128)(2,1)}, u32[]{:S(2)}) copy-start(bf16[4096,1]{0,1:T(2,128)(2,1)} %param.9) | copy-start | bytes 24580
  176.9 52.6 %all-to-all-start.10 = ((f32[16,8,512]{2,1,0:T(8,128)}), f32[16,8,512]{2,1,0:T(8,128)S(1)}, u32[]{:S(2)}, u32[]{:S(2)}) async-start(f32[16,8,512]{2,1,0:T(8,128)} %broadcast_in_dim.33), calls=%async_computation.12 | async-start | bytes 524288 | tf_op jit(solution)/shard_map/all_to_all | solution.py:272
  183.7 41.0 %reduce-scatter.5.cloned.1.call-start = ((), (), s32[]{:S(2)}) async-start(), calls=%async_computation.14 | async-start | bytes 327680 | tf_op jit(solution)/shard_map/reduce_scatter | solution.py:322
  224.7 10.3 %collective-permute-start.4 = (bf16[256,128]{1,0:T(8,128)(2,1)}, bf16[256,128]{1,0:T(8,128)(2,1)S(1)}, u32[]{:S(2)}, u32[]{:S(2)}) collective-permute-start(bf16[256,128]{1,0:T(8,128)(2,1)} %reduce-scatter.5.cloned.1.call-done), channel_id=1, source_target_pairs={{0,0},{1,128},{2,256},{3,384},{128,1},{129,129},{130,257},{131,385... | collective-permute-start | bytes 196616 | tf_op jit(solution)/shard_map/ppermute | solution.py:323
  229.6 6.0 %collective-permute-start.5 = (f32[8,512]{1,0:T(8,128)S(1)}, f32[8,512]{1,0:T(8,128)S(1)}, u32[]{:S(2)}, u32[]{:S(2)}) collective-permute-start(f32[8,512]{1,0:T(8,128)S(1)} %reduce_sum.19), channel_id=1, source_target_pairs={{0,16},{16,0},{1,17},{17,1},{2,18},{18,2},{3,19},{19,3},{4,20},{20... | collective-permute-start | bytes 49160 | tf_op jit(solution)/shard_map/ppermute | solution.py:344
Sparse Core Ops, SparseCore 0:
  128.1 25.1 reduce-scatter.2
  187.6 37.0 reduce-scatter.4

commit v2 on v1

--- a/solution.py
+++ b/solution.py
@@ -14,9 +14,9 @@
 LIMIT = 32 * 1024 * 1024
 
 
-def call(body, outs, vmem_args, smem_args=(), flops=0):
+def call(body, outs, vmem_args, smem_args=(), flops=0, any_args=(), scratch=()):
     multi = isinstance(outs, (list, tuple))
-    arrays = list(smem_args) + list(vmem_args)
+    arrays = list(smem_args) + list(vmem_args) + list(any_args)
     nbytes = sum(a.size * a.dtype.itemsize for a in arrays)
     for o in outs if multi else [outs]:
         nbytes += o.size * o.dtype.itemsize
@@ -25,8 +25,9 @@
     return pl.pallas_call(
         body,
         out_shape=outs,
-        in_specs=[sm] * len(smem_args) + [vm] * len(vmem_args),
+        in_specs=[sm] * len(smem_args) + [vm] * len(vmem_args) + [pl.BlockSpec(memory_space=pl.ANY)] * len(any_args),
         out_specs=[vm] * len(outs) if multi else vm,
+        scratch_shapes=list(scratch),
         compiler_params=pltpu.CompilerParams(vmem_limit_bytes=LIMIT),
         cost_estimate=pl.CostEstimate(flops=flops, bytes_accessed=nbytes, transcendentals=0),
     )(*arrays)
@@ -68,9 +69,14 @@
     return top, factors, total
 
 
-def partial_body(kind, tok, grd, route, out, logit):
+def partial_body(kind, route, tok_hbm, grd_hbm, out, logit, tok, grd, sems):
+    loads = [pltpu.make_async_copy(tok_hbm.at[s], tok.at[s], sems.at[s]) for s in range(4)]
+    loads += [pltpu.make_async_copy(grd_hbm.at[s], grd.at[s], sems.at[4 + s]) for s in range(4)]
+    for load in loads:
+        load.start()
     ls = []
     for s in range(4):
+        loads[s].wait()
         acc = jnp.zeros((32, 512), F32)
         for j in range(8):
             d = slice(j * 512, j * 512 + 512)
@@ -88,6 +94,8 @@
         sums.append((ws[0] + ws[1]) + (ws[2] + ws[3]))
         weights.append(ws)
     stats = pack_stats(jnp.concatenate(tops, 0), jnp.concatenate(sums, 0))
+    for s in range(4):
+        loads[4 + s].wait()
     for y in range(NY):
         for j in range(4):
             out[y, 128:144, j * 128 : j * 128 + 128] = stats[j * 16 : j * 16 + 16]
@@ -185,7 +193,7 @@
             ).astype(BF)
 
 
-def weight_grad_body(mixed, mixed_other, inner, inner_other, out):
+def weight_grad_body(place, mixed, mixed_other, inner, inner_other, out):
     act = jnp.concatenate([inner[:64], inner_other[:64]], 0)
     dpre = jnp.concatenate([inner[64:], inner_other[64:]], 0)
     for h in range(NH):
@@ -194,8 +202,9 @@
         gin = lax.dot_general(mix, dpre, (((0,), (0,)), ((), ())), preferred_element_type=F32)
         gout = lax.dot_general(act, dmo, (((0,), (0,)), ((), ())), preferred_element_type=F32)
         for a in range(NX):
-            out[a, h, :128] = gin[:, a * 128 : a * 128 + 128].astype(BF)
-            out[a, h, 128:] = gout[a * 128 : a * 128 + 128].astype(BF)
+            to = lax.rem(a + NX - place[0], NX)
+            out[h, to, :128] = gin[:, a * 128 : a * 128 + 128].astype(BF)
+            out[h, to, 128:] = gout[a * 128 : a * 128 + 128].astype(BF)
 
 
 def sum_four_body(got, out):
@@ -277,23 +286,26 @@
     flip = [(a * 4 + b, b * 4 + a) for a in range(4) for b in range(4)]
     cores = [(0, 1), (1, 0)]
 
+    mine = group * 4 + jnp.arange(4, dtype=jnp.int32)
+    kind = jnp.any(members[0, 32:][None, :] == mine[:, None], axis=1).astype(jnp.int32)
+    route = router.reshape(1, 4096)
+
+    sent, logit = call(
+        partial_body,
+        [sds((NY, 144, 1024)), sds((4, 32, 128), F32)],
+        (route,),
+        (kind,),
+        flops=10_000_000,
+        any_args=(tokens, grad_out),
+        scratch=(pltpu.VMEM((4, 32, 4096), BF), pltpu.VMEM((4, 32, 4096), BF), pltpu.SemaphoreType.DMA((8,))),
+    )
     shard = jnp.concatenate([w_in[0], w_out[0]], axis=0)
     shard = lax.ppermute(shard, ("x", "y"), flip)
+    sent, shard = lax.optimization_barrier((sent, shard))
     shard = lax.all_gather(shard, "zh", axis=0, tiled=False)
     shard = swap(jnp.broadcast_to(shard[None], (NX, NH, 256, 128)), "x")
     other = lax.ppermute(shard, "core", cores)
 
-    mine = group * 4 + jnp.arange(4, dtype=jnp.int32)
-    kind = jnp.any(members[0, 32:][None, :] == mine[:, None], axis=1).astype(jnp.int32)
-    route = router.reshape(1, 4096)
-
-    sent, logit = call(
-        partial_body,
-        [sds((NY, 144, 1024)), sds((4, 32, 128), F32)],
-        (tokens, grad_out, route),
-        (kind,),
-        flops=10_000_000,
-    )
     sent = call(over_y_body, sds((NL, 160, 256)), (swap(sent, "y"),), flops=1_000_000)
     sent, final = call(
         over_zl_body, [sds((NL, 128, 256)), sds((64, 128), F32)], (swap(sent, "zl"),), flops=300_000
@@ -304,10 +316,11 @@
     mixed_other = lax.ppermute(half, "core", cores)
 
     sent = call(hidden_body, sds((NY, 128, 512)), (mixed, shard, other), (core_s,), flops=140_000_000)
+    got, mixed_other = lax.optimization_barrier((swap(sent, "y"), mixed_other))
     sent, inner = call(
         expert_body,
         [sds((NL, 128, 256)), sds((128, 512))],
-        (swap(sent, "y"), shard, other),
+        (got, shard, other),
         (core_s,),
         flops=140_000_000,
     )
@@ -316,13 +329,13 @@
         weight_grad_body,
         sds((NX, NH, 256, 128)),
         (mixed_half, mixed_other, inner, inner_other),
+        (jnp.full((1,), lax.axis_index("x"), jnp.int32),),
         flops=140_000_000,
     )
-    grads = lax.psum_scatter(grads.reshape(NX * NH * 256, 128), "x", scatter_dimension=0, tiled=True)
-    grads = lax.psum_scatter(grads, "zh", scatter_dimension=0, tiled=True)
-    grads = lax.ppermute(grads, ("x", "y"), flip)
-
-    sent = call(sum_four_body, sds((NL, 128, 256)), (swap(sent, "zl"),), flops=300_000)
+    got, grads = lax.optimization_barrier((swap(sent, "zl"), grads))
+    grads = lax.psum_scatter(grads.reshape(NX * NH * 256, 128), "zh", scatter_dimension=0, tiled=True)
+
+    sent = call(sum_four_body, sds((NL, 128, 256)), (got,), flops=300_000)
     sent = swap(sent, "zl")
     back = swap(jnp.broadcast_to(sent[None], (NY, NL, 128, 256)), "y")
     sent, dmix = call(
@@ -339,8 +352,20 @@
         (kind,),
         flops=5_000_000,
     )
-    droute = jnp.sum(swap(droute, ("x", "y")), axis=0)
-    droute = jnp.sum(swap(jnp.broadcast_to(droute[None], (16, 8, 512)), ("zh", "zl")), axis=0)
+    droute, grads = lax.optimization_barrier((swap(droute, ("x", "y")), grads))
+    droute = jnp.sum(droute, axis=0)
+    droute = swap(jnp.broadcast_to(droute[None], (16, 8, 512)), ("zh", "zl"))
+    grads = grads.reshape(NX, 256, 128)
+    parts = [
+        lax.ppermute(
+            grads[i], ("x", "y"), [(x * NY + y, y * NY + (x + i) % NX) for x in range(NX) for y in range(NY)]
+        )
+        for i in range(NX)
+    ]
+    droute, parts = lax.optimization_barrier((droute, parts))
+    parts = [p.astype(F32) for p in parts]
+    grads = ((parts[0] + parts[1]) + (parts[2] + parts[3])).astype(BF)
+    droute = jnp.sum(droute, axis=0)
     droute = droute + lax.ppermute(droute, "core", cores)
     return grad_tokens, grads[None, :128], grads[None, 128:], droute.reshape(4096, 1)
 

time: 244 us -> 221 us (0.906)
  the two profiles are of different devices: /device:TPU:4 before, /device:TPU:1 now
where the time goes in v2:
time: 221 us; the launch traced here: 217 us
  blocking collectives  81.6 us (37%)
  starting transfers between devices  75.5 us (34%)
  waiting for transfers between devices  23.8 us (11%)
  between operations  14.3 us (6%)
  Pallas kernels  13.5 us (6%)
  local copies, waits for them, and re-layouts  7.23 us (3%)
    all_to_all x4, blocking collectives, swap(): return lax.all_to_all(value, axes, split_axis=0, concat_axis=0, tiled=True)  57.1 us
    all_to_all x7, starting transfers between devices, swap(): return lax.all_to_all(value, axes, split_axis=0, concat_axis=0, tiled=True)  38.2 us
    all_gather x1, blocking collectives, shards(): shard = lax.all_gather(shard, 'zh', axis=0, tiled=False)  24.5 us
    all_to_all x7, waiting for transfers between devices, swap(): return lax.all_to_all(value, axes, split_axis=0, concat_axis=0, tiled=True)  16 us
    pallas_call x9, Pallas kernels, call(): pl.pallas_call(body, out_shape=outs, in_specs=[sm] * len(smem_args) + [vm...  13.5 us
    ppermute x4, starting transfers between devices, shards(): lax.ppermute(grads[i], ('x', 'y'), [(x * NY + y, y * NY + (x + i) % NX) f...  9.24 us
    ppermute x1, starting transfers between devices, shards(): mixed_other = lax.ppermute(half, 'core', cores)  7.52 us
    ppermute x1, starting transfers between devices, shards(): inner_other = lax.ppermute(inner, 'core', cores)  7.07 us
  transfers between devices with their start and end apart: 17, of which 6 were waited for; matrix products, arithmetic and copies ran while one was open for 1% of the time, Pallas kernels for 5%

profile of v2, /device:TPU:1, one launch (start us, length us, event | category | flops | bytes accessed | tf_op | source)
XLA Modules:
  0.0 216.9 jit_solution(15645972127363739139)
XLA Ops:
  9.6 1.2 copy-done
  10.8 1.2 copy-done.2
  12.7 3.2 %shard_map.93 = (bf16[4,144,1024]{2,1,0:T(8,128)(2,1)}, f32[4,32,128]{2,1,0:T(8,128)S(1)}) custom-call(s32[4]{0:T(128)S(1)} %convert_element_type.18.kind, bf16[1,4096]{1,0:T(2,128)(2,1)S(1)} %bitcast.18, bf16[4,32,4096]{2,1,0:T(8,128)(2,1)S(1)} %copy-done, bf16[4,32,4096]{2,1,0:T(8,128)(2,1)S(1)} %copy-done.2), custom_call_target="tpu_custom_call" | custom-call | flops 10000000 | bytes 3350544 | tf_op jit(solution)/shard_map/pallas_call | solution.py:25
  15.9 8.8 %all-to-all-start = ((bf16[4,144,1024]{2,1,0:T(8,128)(2,1)}), bf16[4,144,1024]{2,1,0:T(8,128)(2,1)S(1)}, u32[]{:S(2)}, u32[]{:S(2)}) async-start(bf16[4,144,1024]{2,1,0:T(8,128)(2,1)} %get-tuple-element.28), calls=%async_computation | async-start | bytes 2359296 | tf_op jit(solution)/shard_map/all_to_all | solution.py:281
  24.7 24.5 %all-gather = bf16[1024,128]{1,0:T(8,128)(2,1)S(1)} all-gather(bf16[256,128]{1,0:T(8,128)(2,1)S(1)} %collective-permute-done), channel_id=2, replica_groups=mesh['x'=4,'zh'=4,'core'=2,'zl'=4,'y'=4] {'zh'}, dimensions={0}, use_global_device_ids=true | all-gather | bytes 327680 | tf_op jit(solution)/shard_map/all_gather | solution.py:305
  49.1 1.2 broadcast_in_dim.15
  50.3 3.6 %all-to-all-start.3 = ((bf16[4,4,256,128]{3,2,1,0:T(8,128)(2,1)}), bf16[4,4,256,128]{3,2,1,0:T(8,128)(2,1)S(1)}, u32[]{:S(2)}, u32[]{:S(2)}) async-start(bf16[4,4,256,128]{3,2,1,0:T(8,128)(2,1)} %broadcast_in_dim.15), calls=%async_computation.3 | async-start | bytes 2097152 | tf_op jit(solution)/shard_map/all_to_all | solution.py:281
  54.0 1.1 shard_map.94
  55.1 10.4 %all-to-all-done.3.own = bf16[4,4,256,128]{3,2,1,0:T(8,128)(2,1)S(1)} async-done(((bf16[4,4,256,128]{3,2,1,0:T(8,128)(2,1)}), bf16[4,4,256,128]{3,2,1,0:T(8,128)(2,1)S(1)}, u32[]{:S(2)}, u32[]{:S(2)}) %all-to-all-start.3) | async-done | bytes 1048608 | tf_op jit(solution)/shard_map/all_to_all | solution.py:281
  65.4 3.5 %all-to-all-start.1 = ((bf16[4,160,256]{2,1,0:T(8,128)(2,1)}), bf16[4,160,256]{2,1,0:T(8,128)(2,1)S(1)}, u32[]{:S(2)}, u32[]{:S(2)}) async-start(bf16[4,160,256]{2,1,0:T(8,128)(2,1)} %shard_map.94), calls=%async_computation.1 | async-start | bytes 655360 | tf_op jit(solution)/shard_map/all_to_all | solution.py:281
  68.9 6.5 %collective-permute-start.1 = (bf16[4,4,256,128]{3,2,1,0:T(8,128)(2,1)S(1)}, bf16[4,4,256,128]{3,2,1,0:T(8,128)(2,1)S(1)}, u32[]{:S(2)}, u32[]{:S(2)}) collective-permute-start(bf16[4,4,256,128]{3,2,1,0:T(8,128)(2,1)S(1)} %all-to-all-done.3.own), channel_id=1, source_target_pairs={{0,16},{16,0},{1,17},{17,1},{2,18},{18,2},{3,19},{19,3},{4,20},{20... | collective-permute-start | bytes 3145736 | tf_op jit(solution)/shard_map/ppermute | solution.py:307
  76.4 4.8 %all-to-all-start.2 = ((bf16[4,128,256]{2,1,0:T(8,128)(2,1)}), bf16[4,128,256]{2,1,0:T(8,128)(2,1)S(1)}, u32[]{:S(2)}, u32[]{:S(2)}) async-start(bf16[4,128,256]{2,1,0:T(8,128)(2,1)} %get-tuple-element.29), calls=%async_computation.2 | async-start | bytes 524288 | tf_op jit(solution)/shard_map/all_to_all | solution.py:281
  81.2 5.6 %all-to-all-done.2.mixed = bf16[4,128,256]{2,1,0:T(8,128)(2,1)S(1)} async-done(((bf16[4,128,256]{2,1,0:T(8,128)(2,1)}), bf16[4,128,256]{2,1,0:T(8,128)(2,1)S(1)}, u32[]{:S(2)}, u32[]{:S(2)}) %all-to-all-start.2) | async-done | bytes 262176 | tf_op jit(solution)/shard_map/all_to_all | solution.py:281
  86.8 1.5 shard_map.96
  88.3 4.5 %all-to-all-start.4 = ((bf16[4,128,512]{2,1,0:T(8,128)(2,1)}), bf16[4,128,512]{2,1,0:T(8,128)(2,1)S(1)}, u32[]{:S(2)}, u32[]{:S(2)}) async-start(bf16[4,128,512]{2,1,0:T(8,128)(2,1)} %shard_map.96), calls=%async_computation.4 | async-start | bytes 1048576 | tf_op jit(solution)/shard_map/all_to_all | solution.py:281
  92.9 7.5 %collective-permute-start.2 = (bf16[4,128,128]{2,1,0:T(8,128)(2,1)S(1)}, bf16[4,128,128]{2,1,0:T(8,128)(2,1)S(1)}, u32[]{:S(2)}, u32[]{:S(2)}) collective-permute-start(bf16[4,128,128]{2,1,0:T(8,128)(2,1)S(1)} %get-tuple-element.55), channel_id=1, source_target_pairs={{0,16},{16,0},{1,17},{17,1},{2,18},{18,2},{3,19},{19,3},{4,20},{20... | collective-permute-start | bytes 393224 | tf_op jit(solution)/shard_map/ppermute | solution.py:316
  101.3 1.4 shard_map.97
  102.8 3.4 %all-to-all-start.5 = ((bf16[4,128,256]{2,1,0:T(8,128)(2,1)}), bf16[4,128,256]{2,1,0:T(8,128)(2,1)S(1)}, u32[]{:S(2)}, u32[]{:S(2)}) async-start(bf16[4,128,256]{2,1,0:T(8,128)(2,1)} %get-tuple-element.32), calls=%async_computation.5 | async-start | bytes 524288 | tf_op jit(solution)/shard_map/all_to_all | solution.py:281
  106.2 7.1 %collective-permute-start.3 = (bf16[128,512]{1,0:T(8,128)(2,1)S(1)}, bf16[128,512]{1,0:T(8,128)(2,1)S(1)}, u32[]{:S(2)}, u32[]{:S(2)}) collective-permute-start(bf16[128,512]{1,0:T(8,128)(2,1)S(1)} %get-tuple-element.34.inner), channel_id=1, source_target_pairs={{0,16},{16,0},{1,17},{17,1},{2,18},{18,2},{3,19},{19,3},{4,20},{20... | collective-permute-start | bytes 393224 | tf_op jit(solution)/shard_map/ppermute | solution.py:327
  114.3 1.5 shard_map.98
  115.8 11.1 %all_to_all.55 = bf16[4,128,256]{2,1,0:T(8,128)(2,1)S(1)} all-to-all(bf16[4,128,256]{2,1,0:T(8,128)(2,1)S(1)} %shard_map.99), channel_id=1, replica_groups=mesh['x'=4,'zh'=4,'core'=2,'zl'=4,'y'=4] {'zl'}, dimensions={0} | all-to-all | bytes 524288 | tf_op jit(solution)/shard_map/all_to_all | solution.py:281
  127.0 14.4 %all_to_all.56.back = bf16[4,4,128,256]{3,2,1,0:T(8,128)(2,1)S(1)} all-to-all(bf16[4,4,128,256]{3,2,1,0:T(8,128)(2,1)S(1)} %broadcast_in_dim.34), channel_id=1, replica_groups=mesh['x'=4,'zh'=4,'core'=2,'zl'=4,'y'=4] {'y'}, dimensions={0} | all-to-all | bytes 2097152 | tf_op jit(solution)/shard_map/all_to_all | solution.py:281
  141.4 1.2 shard_map.100
  142.7 16.3 %all_to_all.57.got = f32[16,8,128]{2,1,0:T(8,128)S(1)} all-to-all(f32[16,8,128]{2,1,0:T(8,128)S(1)} %get-tuple-element.39), channel_id=1, replica_groups=mesh['x'=4,'zh'=4,'core'=2,'zl'=4,'y'=4] {'zl','y'}, dimensions={0} | all-to-all | bytes 131072 | tf_op jit(solution)/shard_map/all_to_all | solution.py:281
  159.0 2.5 %shard_map.101 = (bf16[4,32,4096]{2,1,0:T(8,128)(2,1)}, f32[16,8,512]{2,1,0:T(8,128)S(1)}) custom-call(s32[4]{0:T(128)S(1)} %convert_element_type.18.kind, bf16[4,32,4096]{2,1,0:T(8,128)(2,1)S(1)} %copy-done.1, bf16[4,4,128,256]{3,2,1,0:T(8,128)(2,1)S(1)} %all_to_all.56.back, f32[4,32,128]{2,1,0:T(8,128)S(1)} %get-tuple-element.36.logit, ...), custom_call_target="tpu_custom_call" | custom-call | flops 5000000 | bytes 3645456 | tf_op jit(solution)/shard_map/pallas_call | solution.py:25
  161.5 15.3 %all_to_all.58 = f32[16,8,512]{2,1,0:T(8,128)S(1)} all-to-all(f32[16,8,512]{2,1,0:T(8,128)S(1)} %get-tuple-element.41), channel_id=1, replica_groups=mesh['x'=4,'zh'=4,'core'=2,'zl'=4,'y'=4] {'x','y'}, dimensions={0} | all-to-all | bytes 524288 | tf_op jit(solution)/shard_map/all_to_all | solution.py:281
  177.6 9.6 %all-to-all-start.10 = ((f32[16,8,512]{2,1,0:T(8,128)}), f32[16,8,512]{2,1,0:T(8,128)S(1)}, u32[]{:S(2)}, u32[]{:S(2)}) async-start(f32[16,8,512]{2,1,0:T(8,128)} %broadcast_in_dim.35), calls=%async_computation.11 | async-start | bytes 524288 | tf_op jit(solution)/shard_map/all_to_all | solution.py:281
  187.2 2.6 %collective-permute-start.7 = (bf16[256,128]{1,0:T(8,128)(2,1)S(1)}, bf16[256,128]{1,0:T(8,128)(2,1)S(1)}, u32[]{:S(2)}, u32[]{:S(2)}) collective-permute-start(bf16[256,128]{1,0:T(8,128)(2,1)S(1)} %get-tuple-element.50), channel_id=1, source_target_pairs={{0,3},{1,131},{2,259},{3,387},{128,0},{129,128},{130,256},{131,384... | collective-permute-start | bytes 196616 | tf_op jit(solution)/shard_map/ppermute | solution.py:360
  189.9 3.9 %collective-permute-start.6 = (bf16[256,128]{1,0:T(8,128)(2,1)S(1)}, bf16[256,128]{1,0:T(8,128)(2,1)S(1)}, u32[]{:S(2)}, u32[]{:S(2)}) collective-permute-start(bf16[256,128]{1,0:T(8,128)(2,1)S(1)} %get-tuple-element.51), channel_id=1, source_target_pairs={{0,2},{1,130},{2,258},{3,386},{128,3},{129,131},{130,259},{131,387... | collective-permute-start | bytes 196616 | tf_op jit(solution)/shard_map/ppermute | solution.py:360
  193.8 2.0 collective-permute-start.5
  196.6 5.7 %collective-permute-done.5 = bf16[256,128]{1,0:T(8,128)(2,1)S(1)} collective-permute-done((bf16[256,128]{1,0:T(8,128)(2,1)S(1)}, bf16[256,128]{1,0:T(8,128)(2,1)S(1)}, u32[]{:S(2)}, u32[]{:S(2)}) %collective-permute-start.5) | collective-permute-done | bytes 65568 | tf_op jit(solution)/shard_map/ppermute | solution.py:360
  202.3 6.3 %collective-permute-start.8 = (f32[8,512]{1,0:T(8,128)S(1)}, f32[8,512]{1,0:T(8,128)S(1)}, u32[]{:S(2)}, u32[]{:S(2)}) collective-permute-start(f32[8,512]{1,0:T(8,128)S(1)} %reduce_sum.19), channel_id=1, source_target_pairs={{0,16},{16,0},{1,17},{17,1},{2,18},{18,2},{3,19},{19,3},{4,20},{20... | collective-permute-start | bytes 49160 | tf_op jit(solution)/shard_map/ppermute | solution.py:369
  (47 shorter events, 9.2 us)
Async XLA Ops:
  7.9 7.9 %collective-permute-start = (bf16[256,128]{1,0:T(8,128)(2,1)S(1)}, bf16[256,128]{1,0:T(8,128)(2,1)S(1)}, u32[]{:S(2)}, u32[]{:S(2)}) collective-permute-start(bf16[256,128]{1,0:T(8,128)(2,1)S(1)} %pad_maximum_fusion), channel_id=1, source_target_pairs={{0,0},{1,128},{2,256},{3,384},{128,1},{129,129},{130,257},{131,385... | collective-permute-start | bytes 196616 | tf_op jit(solution)/shard_map/ppermute | solution.py:303
  9.5 1.2 copy-start
  10.8 1.2 copy-start.2
  12.0 0.7 copy-start.4
  15.9 33.2 %all-to-all-start = ((bf16[4,144,1024]{2,1,0:T(8,128)(2,1)}), bf16[4,144,1024]{2,1,0:T(8,128)(2,1)S(1)}, u32[]{:S(2)}, u32[]{:S(2)}) async-start(bf16[4,144,1024]{2,1,0:T(8,128)(2,1)} %get-tuple-element.28), calls=%async_computation | async-start | bytes 2359296 | tf_op jit(solution)/shard_map/all_to_all | solution.py:281
  50.3 15.1 %all-to-all-start.3 = ((bf16[4,4,256,128]{3,2,1,0:T(8,128)(2,1)}), bf16[4,4,256,128]{3,2,1,0:T(8,128)(2,1)S(1)}, u32[]{:S(2)}, u32[]{:S(2)}) async-start(bf16[4,4,256,128]{3,2,1,0:T(8,128)(2,1)} %broadcast_in_dim.15), calls=%async_computation.3 | async-start | bytes 2097152 | tf_op jit(solution)/shard_map/all_to_all | solution.py:281
  65.4 9.9 %all-to-all-start.1 = ((bf16[4,160,256]{2,1,0:T(8,128)(2,1)}), bf16[4,160,256]{2,1,0:T(8,128)(2,1)S(1)}, u32[]{:S(2)}, u32[]{:S(2)}) async-start(bf16[4,160,256]{2,1,0:T(8,128)(2,1)} %shard_map.94), calls=%async_computation.1 | async-start | bytes 655360 | tf_op jit(solution)/shard_map/all_to_all | solution.py:281
  68.9 12.3 %collective-permute-start.1 = (bf16[4,4,256,128]{3,2,1,0:T(8,128)(2,1)S(1)}, bf16[4,4,256,128]{3,2,1,0:T(8,128)(2,1)S(1)}, u32[]{:S(2)}, u32[]{:S(2)}) collective-permute-start(bf16[4,4,256,128]{3,2,1,0:T(8,128)(2,1)S(1)} %all-to-all-done.3.own), channel_id=1, source_target_pairs={{0,16},{16,0},{1,17},{17,1},{2,18},{18,2},{3,19},{19,3},{4,20},{20... | collective-permute-start | bytes 3145736 | tf_op jit(solution)/shard_map/ppermute | solution.py:307
  76.4 10.4 %all-to-all-start.2 = ((bf16[4,128,256]{2,1,0:T(8,128)(2,1)}), bf16[4,128,256]{2,1,0:T(8,128)(2,1)S(1)}, u32[]{:S(2)}, u32[]{:S(2)}) async-start(bf16[4,128,256]{2,1,0:T(8,128)(2,1)} %get-tuple-element.29), calls=%async_computation.2 | async-start | bytes 524288 | tf_op jit(solution)/shard_map/all_to_all | solution.py:281
  88.3 13.0 %all-to-all-start.4 = ((bf16[4,128,512]{2,1,0:T(8,128)(2,1)}), bf16[4,128,512]{2,1,0:T(8,128)(2,1)S(1)}, u32[]{:S(2)}, u32[]{:S(2)}) async-start(bf16[4,128,512]{2,1,0:T(8,128)(2,1)} %shard_map.96), calls=%async_computation.4 | async-start | bytes 1048576 | tf_op jit(solution)/shard_map/all_to_all | solution.py:281
  92.9 8.5 %collective-permute-start.2 = (bf16[4,128,128]{2,1,0:T(8,128)(2,1)S(1)}, bf16[4,128,128]{2,1,0:T(8,128)(2,1)S(1)}, u32[]{:S(2)}, u32[]{:S(2)}) collective-permute-start(bf16[4,128,128]{2,1,0:T(8,128)(2,1)S(1)} %get-tuple-element.55), channel_id=1, source_target_pairs={{0,16},{16,0},{1,17},{17,1},{2,18},{18,2},{3,19},{19,3},{4,20},{20... | collective-permute-start | bytes 393224 | tf_op jit(solution)/shard_map/ppermute | solution.py:316
  102.8 13.0 %all-to-all-start.5 = ((bf16[4,128,256]{2,1,0:T(8,128)(2,1)}), bf16[4,128,256]{2,1,0:T(8,128)(2,1)S(1)}, u32[]{:S(2)}, u32[]{:S(2)}) async-start(bf16[4,128,256]{2,1,0:T(8,128)(2,1)} %get-tuple-element.32), calls=%async_computation.5 | async-start | bytes 524288 | tf_op jit(solution)/shard_map/all_to_all | solution.py:281
  106.2 70.6 %reduce-scatter.2.cloned.1.call-start = ((), (), s32[]{:S(2)}) async-start(), calls=%async_computation.12 | async-start | bytes 1310720 | tf_op jit(solution)/shard_map/reduce_scatter | solution.py:336
  106.2 8.0 %collective-permute-start.3 = (bf16[128,512]{1,0:T(8,128)(2,1)S(1)}, bf16[128,512]{1,0:T(8,128)(2,1)S(1)}, u32[]{:S(2)}, u32[]{:S(2)}) collective-permute-start(bf16[128,512]{1,0:T(8,128)(2,1)S(1)} %get-tuple-element.34.inner), channel_id=1, source_target_pairs={{0,16},{16,0},{1,17},{17,1},{2,18},{18,2},{3,19},{19,3},{4,20},{20... | collective-permute-start | bytes 393224 | tf_op jit(solution)/shard_map/ppermute | solution.py:327
  127.0 14.4 %copy-start.1 = (bf16[4,32,4096]{2,1,0:T(8,128)(2,1)S(1)}, bf16[4,32,4096]{2,1,0:T(8,128)(2,1)}, u32[]{:S(2)}) copy-start(bf16[4,32,4096]{2,1,0:T(8,128)(2,1)} %tok.3) | copy-start | bytes 3145732
  127.0 14.4 %copy-start.3 = (bf16[4,32,4096]{2,1,0:T(8,128)(2,1)S(1)}, bf16[4,32,4096]{2,1,0:T(8,128)(2,1)}, u32[]{:S(2)}) copy-start(bf16[4,32,4096]{2,1,0:T(8,128)(2,1)} %grd.1) | copy-start | bytes 3145732
  141.4 17.6 %copy-start.5 = (bf16[4096,1]{0,1:T(2,128)(2,1)S(1)}, bf16[4096,1]{0,1:T(2,128)(2,1)}, u32[]{:S(2)}) copy-start(bf16[4096,1]{0,1:T(2,128)(2,1)} %param.9) | copy-start | bytes 24580
  176.8 10.4 %copy-start.6 = (bf16[1024,128]{1,0:T(8,128)(2,1)S(1)}, bf16[1024,128]{1,0:T(8,128)(2,1)}, u32[]{:S(2)}) copy-start(bf16[1024,128]{1,0:T(8,128)(2,1)} %reduce-scatter.2.cloned.1.call-done) | copy-start | bytes 786436
  177.6 24.7 %all-to-all-start.10 = ((f32[16,8,512]{2,1,0:T(8,128)}), f32[16,8,512]{2,1,0:T(8,128)S(1)}, u32[]{:S(2)}, u32[]{:S(2)}) async-start(f32[16,8,512]{2,1,0:T(8,128)} %broadcast_in_dim.35), calls=%async_computation.11 | async-start | bytes 524288 | tf_op jit(solution)/shard_map/all_to_all | solution.py:281
  187.2 9.3 %collective-permute-start.7 = (bf16[256,128]{1,0:T(8,128)(2,1)S(1)}, bf16[256,128]{1,0:T(8,128)(2,1)S(1)}, u32[]{:S(2)}, u32[]{:S(2)}) collective-permute-start(bf16[256,128]{1,0:T(8,128)(2,1)S(1)} %get-tuple-element.50), channel_id=1, source_target_pairs={{0,3},{1,131},{2,259},{3,387},{128,0},{129,128},{130,256},{131,384... | collective-permute-start | bytes 196616 | tf_op jit(solution)/shard_map/ppermute | solution.py:360
  189.9 6.7 %collective-permute-start.6 = (bf16[256,128]{1,0:T(8,128)(2,1)S(1)}, bf16[256,128]{1,0:T(8,128)(2,1)S(1)}, u32[]{:S(2)}, u32[]{:S(2)}) collective-permute-start(bf16[256,128]{1,0:T(8,128)(2,1)S(1)} %get-tuple-element.51), channel_id=1, source_target_pairs={{0,2},{1,130},{2,258},{3,386},{128,3},{129,131},{130,259},{131,387... | collective-permute-start | bytes 196616 | tf_op jit(solution)/shard_map/ppermute | solution.py:360
  193.8 8.4 %collective-permute-start.5 = (bf16[256,128]{1,0:T(8,128)(2,1)S(1)}, bf16[256,128]{1,0:T(8,128)(2,1)S(1)}, u32[]{:S(2)}, u32[]{:S(2)}) collective-permute-start(bf16[256,128]{1,0:T(8,128)(2,1)S(1)} %get-tuple-element.52), channel_id=1, source_target_pairs={{0,1},{1,129},{2,257},{3,385},{128,2},{129,130},{130,258},{131,386... | collective-permute-start | bytes 196616 | tf_op jit(solution)/shard_map/ppermute | solution.py:360
  195.8 6.4 %collective-permute-start.4 = (bf16[256,128]{1,0:T(8,128)(2,1)S(1)}, bf16[256,128]{1,0:T(8,128)(2,1)S(1)}, u32[]{:S(2)}, u32[]{:S(2)}) collective-permute-start(bf16[256,128]{1,0:T(8,128)(2,1)S(1)} %get-tuple-element.53), channel_id=1, source_target_pairs={{0,0},{1,128},{2,256},{3,384},{128,1},{129,129},{130,257},{131,385... | collective-permute-start | bytes 196616 | tf_op jit(solution)/shard_map/ppermute | solution.py:360
  202.3 7.2 %collective-permute-start.8 = (f32[8,512]{1,0:T(8,128)S(1)}, f32[8,512]{1,0:T(8,128)S(1)}, u32[]{:S(2)}, u32[]{:S(2)}) collective-permute-start(f32[8,512]{1,0:T(8,128)S(1)} %reduce_sum.19), channel_id=1, source_target_pairs={{0,16},{16,0},{1,17},{17,1},{2,18},{18,2},{3,19},{19,3},{4,20},{20... | collective-permute-start | bytes 49160 | tf_op jit(solution)/shard_map/ppermute | solution.py:369
Sparse Core Ops, SparseCore 0:
  115.9 53.9 reduce-scatter.1

commit v3 on v2

--- a/solution.py
+++ b/solution.py
@@ -14,7 +14,7 @@
 LIMIT = 32 * 1024 * 1024
 
 
-def call(body, outs, vmem_args, smem_args=(), flops=0, any_args=(), scratch=()):
+def call(body, outs, vmem_args, smem_args=(), flops=0, any_args=(), scratch=(), limit=LIMIT):
     multi = isinstance(outs, (list, tuple))
     arrays = list(smem_args) + list(vmem_args) + list(any_args)
     nbytes = sum(a.size * a.dtype.itemsize for a in arrays)
@@ -26,9 +26,9 @@
         body,
         out_shape=outs,
         in_specs=[sm] * len(smem_args) + [vm] * len(vmem_args) + [pl.BlockSpec(memory_space=pl.ANY)] * len(any_args),
-        out_specs=[vm] * len(outs) if multi else vm,
+        out_specs=[sm if o.dtype == jnp.int32 else vm for o in outs] if multi else vm,
         scratch_shapes=list(scratch),
-        compiler_params=pltpu.CompilerParams(vmem_limit_bytes=LIMIT),
+        compiler_params=pltpu.CompilerParams(vmem_limit_bytes=limit),
         cost_estimate=pl.CostEstimate(flops=flops, bytes_accessed=nbytes, transcendentals=0),
     )(*arrays)
 
@@ -69,11 +69,18 @@
     return top, factors, total
 
 
-def partial_body(kind, route, tok_hbm, grd_hbm, out, logit, tok, grd, sems):
+def partial_body(first, order, route, tok_hbm, grd_hbm, out, logit, kind_out, tok, grd, sems):
     loads = [pltpu.make_async_copy(tok_hbm.at[s], tok.at[s], sems.at[s]) for s in range(4)]
     loads += [pltpu.make_async_copy(grd_hbm.at[s], grd.at[s], sems.at[4 + s]) for s in range(4)]
     for load in loads:
         load.start()
+    kind = []
+    for s in range(4):
+        hits = jnp.int32(0)
+        for j in range(32, 64):
+            hits = hits + (order[0, j] == first[0] + s).astype(jnp.int32)
+        kind_out[s] = hits
+        kind.append(hits)
     ls = []
     for s in range(4):
         loads[s].wait()
@@ -193,7 +200,7 @@
             ).astype(BF)
 
 
-def weight_grad_body(place, mixed, mixed_other, inner, inner_other, out):
+def weight_grad_body(mixed, mixed_other, inner, inner_other, out):
     act = jnp.concatenate([inner[:64], inner_other[:64]], 0)
     dpre = jnp.concatenate([inner[64:], inner_other[64:]], 0)
     for h in range(NH):
@@ -202,9 +209,8 @@
         gin = lax.dot_general(mix, dpre, (((0,), (0,)), ((), ())), preferred_element_type=F32)
         gout = lax.dot_general(act, dmo, (((0,), (0,)), ((), ())), preferred_element_type=F32)
         for a in range(NX):
-            to = lax.rem(a + NX - place[0], NX)
-            out[h, to, :128] = gin[:, a * 128 : a * 128 + 128].astype(BF)
-            out[h, to, 128:] = gout[a * 128 : a * 128 + 128].astype(BF)
+            out[a, h, :128] = gin[:, a * 128 : a * 128 + 128].astype(BF)
+            out[a, h, 128:] = gout[a * 128 : a * 128 + 128].astype(BF)
 
 
 def sum_four_body(got, out):
@@ -286,18 +292,17 @@
     flip = [(a * 4 + b, b * 4 + a) for a in range(4) for b in range(4)]
     cores = [(0, 1), (1, 0)]
 
-    mine = group * 4 + jnp.arange(4, dtype=jnp.int32)
-    kind = jnp.any(members[0, 32:][None, :] == mine[:, None], axis=1).astype(jnp.int32)
     route = router.reshape(1, 4096)
 
-    sent, logit = call(
+    sent, logit, kind = call(
         partial_body,
-        [sds((NY, 144, 1024)), sds((4, 32, 128), F32)],
+        [sds((NY, 144, 1024)), sds((4, 32, 128), F32), sds((4,), jnp.int32)],
         (route,),
-        (kind,),
+        (jnp.full((1,), group * 4, jnp.int32), members),
         flops=10_000_000,
         any_args=(tokens, grad_out),
         scratch=(pltpu.VMEM((4, 32, 4096), BF), pltpu.VMEM((4, 32, 4096), BF), pltpu.SemaphoreType.DMA((8,))),
+        limit=63 * 1024 * 1024,
     )
     shard = jnp.concatenate([w_in[0], w_out[0]], axis=0)
     shard = lax.ppermute(shard, ("x", "y"), flip)
@@ -329,11 +334,10 @@
         weight_grad_body,
         sds((NX, NH, 256, 128)),
         (mixed_half, mixed_other, inner, inner_other),
-        (jnp.full((1,), lax.axis_index("x"), jnp.int32),),
         flops=140_000_000,
     )
     got, grads = lax.optimization_barrier((swap(sent, "zl"), grads))
-    grads = lax.psum_scatter(grads.reshape(NX * NH * 256, 128), "zh", scatter_dimension=0, tiled=True)
+    grads = lax.psum_scatter(grads.reshape(NX * NH * 256, 128), "x", scatter_dimension=0, tiled=True)
 
     sent = call(sum_four_body, sds((NL, 128, 256)), (got,), flops=300_000)
     sent = swap(sent, "zl")
@@ -345,6 +349,8 @@
         (kind,),
         flops=5_000_000,
     )
+    sent, grads = lax.optimization_barrier((sent, grads))
+    grads = lax.psum_scatter(grads, "zh", scatter_dimension=0, tiled=True)
     grad_tokens, droute = call(
         final_body,
         [sds((4, 32, 4096)), sds((16, 8, 512), F32)],
@@ -352,21 +358,13 @@
         (kind,),
         flops=5_000_000,
     )
-    droute, grads = lax.optimization_barrier((swap(droute, ("x", "y")), grads))
+    droute = jnp.sum(swap(droute, ("x", "y")), axis=0)
+    droute = droute + lax.ppermute(droute, "core", cores)
+    droute, grads = lax.optimization_barrier((droute, grads))
+    droute = swap(jnp.broadcast_to(droute[None], (16, 8, 512)), ("zh", "zl"))
+    grads = lax.ppermute(grads, ("x", "y"), flip)
+    droute, grads = lax.optimization_barrier((droute, grads))
     droute = jnp.sum(droute, axis=0)
-    droute = swap(jnp.broadcast_to(droute[None], (16, 8, 512)), ("zh", "zl"))
-    grads = grads.reshape(NX, 256, 128)
-    parts = [
-        lax.ppermute(
-            grads[i], ("x", "y"), [(x * NY + y, y * NY + (x + i) % NX) for x in range(NX) for y in range(NY)]
-        )
-        for i in range(NX)
-    ]
-    droute, parts = lax.optimization_barrier((droute, parts))
-    parts = [p.astype(F32) for p in parts]
-    grads = ((parts[0] + parts[1]) + (parts[2] + parts[3])).astype(BF)
-    droute = jnp.sum(droute, axis=0)
-    droute = droute + lax.ppermute(droute, "core", cores)
     return grad_tokens, grads[None, :128], grads[None, 128:], droute.reshape(4096, 1)
 
 

time: 221 us -> 214 us (0.968)
  the two profiles are of different devices: /device:TPU:1 before, /device:TPU:2 now
where the time goes in v3:
time: 214 us; the launch traced here: 213 us
  blocking collectives  78.7 us (37%)
  waiting for transfers between devices  51.9 us (24%)
  starting transfers between devices  49.2 us (23%)
  Pallas kernels  14.5 us (7%)
  between operations  14.2 us (7%)
  local copies, waits for them, and re-layouts  3.33 us (2%)
    all_to_all x4, blocking collectives, swap(): return lax.all_to_all(value, axes, split_axis=0, concat_axis=0, tiled=True)  52 us
    all_to_all x7, waiting for transfers between devices, swap(): return lax.all_to_all(value, axes, split_axis=0, concat_axis=0, tiled=True)  38.4 us
    all_to_all x7, starting transfers between devices, swap(): return lax.all_to_all(value, axes, split_axis=0, concat_axis=0, tiled=True)  34.6 us
    all_gather x1, blocking collectives, shards(): shard = lax.all_gather(shard, 'zh', axis=0, tiled=False)  26.7 us
    pallas_call x9, Pallas kernels, call(): pl.pallas_call(body, out_shape=outs, in_specs=[sm] * len(smem_args) + [vm...  14.5 us
    reduce_scatter x1, waiting for transfers between devices, shards(): grads = lax.psum_scatter(grads, 'zh', scatter_dimension=0, tiled=True)  5.82 us
  transfers between devices with their start and end apart: 15, of which 11 were waited for; matrix products, arithmetic and copies ran while one was open for 0% of the time, Pallas kernels for 5%

profile of v3, /device:TPU:2, one launch (start us, length us, event | category | flops | bytes accessed | tf_op | source)
XLA Modules:
  0.0 212.6 jit_solution(469717684052492816)
XLA Ops:
  7.9 3.4 %collective-permute-start = (bf16[256,128]{1,0:T(8,128)(2,1)S(1)}, bf16[256,128]{1,0:T(8,128)(2,1)S(1)}, u32[]{:S(2)}, u32[]{:S(2)}) collective-permute-start(bf16[256,128]{1,0:T(8,128)(2,1)S(1)} %pad_maximum_fusion), channel_id=1, source_target_pairs={{0,0},{1,128},{2,256},{3,384},{128,1},{129,129},{130,257},{131,385... | collective-permute-start | bytes 196616 | tf_op jit(solution)/shard_map/ppermute | solution.py:308
  11.4 4.2 %shard_map.93 = (bf16[4,144,1024]{2,1,0:T(8,128)(2,1)}, f32[4,32,128]{2,1,0:T(8,128)}, s32[4]{0:T(128)}) custom-call(s32[1]{0:T(128)} %bitcast.first, s32[1,64]{1,0:T(1,128)} %order.1, bf16[1,4096]{1,0:T(2,128)(2,1)} %bitcast.15, bf16[4,32,4096]{2,1,0:T(8,128)(2,1)} %tok.3, bf16[4,32,4096]{2,1,0:T(8,128)(2,1)} %grd.1), custom_call_target="tpu_custom_call" | custom-call | flops 10000000 | bytes 3350804 | tf_op jit(solution)/shard_map/pallas_call | solution.py:25
  15.6 6.7 %all-to-all-start = ((bf16[4,144,1024]{2,1,0:T(8,128)(2,1)}), bf16[4,144,1024]{2,1,0:T(8,128)(2,1)S(1)}, u32[]{:S(2)}, u32[]{:S(2)}) async-start(bf16[4,144,1024]{2,1,0:T(8,128)(2,1)} %get-tuple-element.29), calls=%async_computation | async-start | bytes 2359296 | tf_op jit(solution)/shard_map/all_to_all | solution.py:287
  22.3 26.7 %all-gather = bf16[1024,128]{1,0:T(8,128)(2,1)S(1)} all-gather(bf16[256,128]{1,0:T(8,128)(2,1)S(1)} %collective-permute-done), channel_id=2, replica_groups=mesh['x'=4,'zh'=4,'core'=2,'zl'=4,'y'=4] {'zh'}, dimensions={0}, use_global_device_ids=true | all-gather | bytes 327680 | tf_op jit(solution)/shard_map/all_gather | solution.py:310
  50.2 6.1 %all-to-all-start.3 = ((bf16[4,4,256,128]{3,2,1,0:T(8,128)(2,1)}), bf16[4,4,256,128]{3,2,1,0:T(8,128)(2,1)S(1)}, u32[]{:S(2)}, u32[]{:S(2)}) async-start(bf16[4,4,256,128]{3,2,1,0:T(8,128)(2,1)} %broadcast_in_dim.32), calls=%async_computation.3 | async-start | bytes 2097152 | tf_op jit(solution)/shard_map/all_to_all | solution.py:287
  57.4 8.3 %all-to-all-done.3.own = bf16[4,4,256,128]{3,2,1,0:T(8,128)(2,1)S(1)} async-done(((bf16[4,4,256,128]{3,2,1,0:T(8,128)(2,1)}), bf16[4,4,256,128]{3,2,1,0:T(8,128)(2,1)S(1)}, u32[]{:S(2)}, u32[]{:S(2)}) %all-to-all-start.3) | async-done | bytes 1048608 | tf_op jit(solution)/shard_map/all_to_all | solution.py:287
  65.7 3.5 %all-to-all-start.1 = ((bf16[4,160,256]{2,1,0:T(8,128)(2,1)}), bf16[4,160,256]{2,1,0:T(8,128)(2,1)S(1)}, u32[]{:S(2)}, u32[]{:S(2)}) async-start(bf16[4,160,256]{2,1,0:T(8,128)(2,1)} %shard_map.94), calls=%async_computation.1 | async-start | bytes 655360 | tf_op jit(solution)/shard_map/all_to_all | solution.py:287
  69.2 1.9 collective-permute-start.1
  71.1 5.3 %all-to-all-done.1.got = bf16[4,160,256]{2,1,0:T(8,128)(2,1)S(1)} async-done(((bf16[4,160,256]{2,1,0:T(8,128)(2,1)}), bf16[4,160,256]{2,1,0:T(8,128)(2,1)S(1)}, u32[]{:S(2)}, u32[]{:S(2)}) %all-to-all-start.1) | async-done | bytes 327712 | tf_op jit(solution)/shard_map/all_to_all | solution.py:287
  77.5 3.6 %all-to-all-start.2 = ((bf16[4,128,256]{2,1,0:T(8,128)(2,1)}), bf16[4,128,256]{2,1,0:T(8,128)(2,1)S(1)}, u32[]{:S(2)}, u32[]{:S(2)}) async-start(bf16[4,128,256]{2,1,0:T(8,128)(2,1)} %get-tuple-element.30), calls=%async_computation.2 | async-start | bytes 524288 | tf_op jit(solution)/shard_map/all_to_all | solution.py:287
  81.1 6.8 %all-to-all-done.2.mixed = bf16[4,128,256]{2,1,0:T(8,128)(2,1)S(1)} async-done(((bf16[4,128,256]{2,1,0:T(8,128)(2,1)}), bf16[4,128,256]{2,1,0:T(8,128)(2,1)S(1)}, u32[]{:S(2)}, u32[]{:S(2)}) %all-to-all-start.2) | async-done | bytes 262176 | tf_op jit(solution)/shard_map/all_to_all | solution.py:287
  87.8 1.5 shard_map.96
  89.4 4.7 %all-to-all-start.4 = ((bf16[4,128,512]{2,1,0:T(8,128)(2,1)}), bf16[4,128,512]{2,1,0:T(8,128)(2,1)S(1)}, u32[]{:S(2)}, u32[]{:S(2)}) async-start(bf16[4,128,512]{2,1,0:T(8,128)(2,1)} %shard_map.96), calls=%async_computation.4 | async-start | bytes 1048576 | tf_op jit(solution)/shard_map/all_to_all | solution.py:287
  94.1 1.9 collective-permute-start.2
  96.0 1.3 collective-permute-done.2.mixed_other
  97.4 4.8 %all-to-all-done.4.got = bf16[4,128,512]{2,1,0:T(8,128)(2,1)S(1)} async-done(((bf16[4,128,512]{2,1,0:T(8,128)(2,1)}), bf16[4,128,512]{2,1,0:T(8,128)(2,1)S(1)}, u32[]{:S(2)}, u32[]{:S(2)}) %all-to-all-start.4) | async-done | bytes 524320 | tf_op jit(solution)/shard_map/all_to_all | solution.py:287
  102.2 1.4 shard_map.97
  103.6 3.4 %all-to-all-start.5 = ((bf16[4,128,256]{2,1,0:T(8,128)(2,1)}), bf16[4,128,256]{2,1,0:T(8,128)(2,1)S(1)}, u32[]{:S(2)}, u32[]{:S(2)}) async-start(bf16[4,128,256]{2,1,0:T(8,128)(2,1)} %get-tuple-element.33), calls=%async_computation.5 | async-start | bytes 524288 | tf_op jit(solution)/shard_map/all_to_all | solution.py:287
  107.0 1.9 collective-permute-start.3
  110.3 1.4 shard_map.98
  111.7 2.1 all-to-all-done.5.got
  113.9 12.0 %all_to_all.55 = bf16[4,128,256]{2,1,0:T(8,128)(2,1)S(1)} all-to-all(bf16[4,128,256]{2,1,0:T(8,128)(2,1)S(1)} %shard_map.99), channel_id=1, replica_groups=mesh['x'=4,'zh'=4,'core'=2,'zl'=4,'y'=4] {'zl'}, dimensions={0} | all-to-all | bytes 524288 | tf_op jit(solution)/shard_map/all_to_all | solution.py:287
  126.0 15.4 %all_to_all.56.back = bf16[4,4,128,256]{3,2,1,0:T(8,128)(2,1)S(1)} all-to-all(bf16[4,4,128,256]{3,2,1,0:T(8,128)(2,1)S(1)} %broadcast_in_dim.33), channel_id=1, replica_groups=mesh['x'=4,'zh'=4,'core'=2,'zl'=4,'y'=4] {'y'}, dimensions={0} | all-to-all | bytes 2097152 | tf_op jit(solution)/shard_map/all_to_all | solution.py:287
  142.8 13.7 %all_to_all.57.got = f32[16,8,128]{2,1,0:T(8,128)S(1)} all-to-all(f32[16,8,128]{2,1,0:T(8,128)S(1)} %get-tuple-element.42), channel_id=1, replica_groups=mesh['x'=4,'zh'=4,'core'=2,'zl'=4,'y'=4] {'zl','y'}, dimensions={0} | all-to-all | bytes 131072 | tf_op jit(solution)/shard_map/all_to_all | solution.py:287
  156.5 2.5 %shard_map.101 = (bf16[4,32,4096]{2,1,0:T(8,128)(2,1)}, f32[16,8,512]{2,1,0:T(8,128)S(1)}) custom-call(s32[4]{0:T(128)S(1)} %copy-done.4, bf16[4,32,4096]{2,1,0:T(8,128)(2,1)S(1)} %copy-done, bf16[4,4,128,256]{3,2,1,0:T(8,128)(2,1)S(1)} %all_to_all.56.back, f32[4,32,128]{2,1,0:T(8,128)S(1)} %copy-done.2, f32[64,128]{1,0:T(8,128)S(1)} %get-tuple-element.38.final, ...), custom_call_target="tpu_custom_call" | custom-call | flops 5000000 | bytes 3645456 | tf_op jit(solution)/shard_map/pallas_call | solution.py:25
  159.0 10.9 %all_to_all.58 = f32[16,8,512]{2,1,0:T(8,128)S(1)} all-to-all(f32[16,8,512]{2,1,0:T(8,128)S(1)} %get-tuple-element.44), channel_id=1, replica_groups=mesh['x'=4,'zh'=4,'core'=2,'zl'=4,'y'=4] {'x','y'}, dimensions={0} | all-to-all | bytes 524288 | tf_op jit(solution)/shard_map/all_to_all | solution.py:287
  169.9 1.9 collective-permute-start.4
  173.0 5.8 %reduce-scatter.5.cloned.1.call-done = bf16[256,128]{1,0:T(8,128)(2,1)} async-done(((bf16[1024,128]{1,0:T(8,128)(2,1)}), bf16[256,128]{1,0:T(8,128)(2,1)}) %reduce-scatter.5.cloned.1.call-update) | async-done | bytes 65552 | tf_op jit(solution)/shard_map/reduce_scatter | solution.py:353
  179.5 6.6 %all-to-all-start.10 = ((f32[16,8,512]{2,1,0:T(8,128)}), f32[16,8,512]{2,1,0:T(8,128)S(1)}, u32[]{:S(2)}, u32[]{:S(2)}) async-start(f32[16,8,512]{2,1,0:T(8,128)} %broadcast_in_dim.34), calls=%async_computation.12 | async-start | bytes 524288 | tf_op jit(solution)/shard_map/all_to_all | solution.py:287
  186.2 3.4 %collective-permute-start.5 = (bf16[256,128]{1,0:T(8,128)(2,1)}, bf16[256,128]{1,0:T(8,128)(2,1)S(1)}, u32[]{:S(2)}, u32[]{:S(2)}) collective-permute-start(bf16[256,128]{1,0:T(8,128)(2,1)} %reduce-scatter.5.cloned.1.call-done), channel_id=1, source_target_pairs={{0,0},{1,128},{2,256},{3,384},{128,1},{129,129},{130,257},{131,385... | collective-permute-start | bytes 196616 | tf_op jit(solution)/shard_map/ppermute | solution.py:365
  189.6 3.9 %collective-permute-done.5 = bf16[256,128]{1,0:T(8,128)(2,1)S(1)} collective-permute-done((bf16[256,128]{1,0:T(8,128)(2,1)}, bf16[256,128]{1,0:T(8,128)(2,1)S(1)}, u32[]{:S(2)}, u32[]{:S(2)}) %collective-permute-start.5) | collective-permute-done | bytes 65568 | tf_op jit(solution)/shard_map/ppermute | solution.py:365
  193.4 11.1 %all-to-all-done.10 = f32[16,8,512]{2,1,0:T(8,128)S(1)} async-done(((f32[16,8,512]{2,1,0:T(8,128)}), f32[16,8,512]{2,1,0:T(8,128)S(1)}, u32[]{:S(2)}, u32[]{:S(2)}) %all-to-all-start.10) | async-done | bytes 262176 | tf_op jit(solution)/shard_map/all_to_all | solution.py:287
  (34 shorter events, 10.2 us)
Async XLA Ops:
  7.9 7.7 %collective-permute-start = (bf16[256,128]{1,0:T(8,128)(2,1)S(1)}, bf16[256,128]{1,0:T(8,128)(2,1)S(1)}, u32[]{:S(2)}, u32[]{:S(2)}) collective-permute-start(bf16[256,128]{1,0:T(8,128)(2,1)S(1)} %pad_maximum_fusion), channel_id=1, source_target_pairs={{0,0},{1,128},{2,256},{3,384},{128,1},{129,129},{130,257},{131,385... | collective-permute-start | bytes 196616 | tf_op jit(solution)/shard_map/ppermute | solution.py:308
  15.6 33.4 %all-to-all-start = ((bf16[4,144,1024]{2,1,0:T(8,128)(2,1)}), bf16[4,144,1024]{2,1,0:T(8,128)(2,1)S(1)}, u32[]{:S(2)}, u32[]{:S(2)}) async-start(bf16[4,144,1024]{2,1,0:T(8,128)(2,1)} %get-tuple-element.29), calls=%async_computation | async-start | bytes 2359296 | tf_op jit(solution)/shard_map/all_to_all | solution.py:287
  50.2 15.5 %all-to-all-start.3 = ((bf16[4,4,256,128]{3,2,1,0:T(8,128)(2,1)}), bf16[4,4,256,128]{3,2,1,0:T(8,128)(2,1)S(1)}, u32[]{:S(2)}, u32[]{:S(2)}) async-start(bf16[4,4,256,128]{3,2,1,0:T(8,128)(2,1)} %broadcast_in_dim.32), calls=%async_computation.3 | async-start | bytes 2097152 | tf_op jit(solution)/shard_map/all_to_all | solution.py:287
  65.7 10.7 %all-to-all-start.1 = ((bf16[4,160,256]{2,1,0:T(8,128)(2,1)}), bf16[4,160,256]{2,1,0:T(8,128)(2,1)S(1)}, u32[]{:S(2)}, u32[]{:S(2)}) async-start(bf16[4,160,256]{2,1,0:T(8,128)(2,1)} %shard_map.94), calls=%async_computation.1 | async-start | bytes 655360 | tf_op jit(solution)/shard_map/all_to_all | solution.py:287
  69.2 11.9 %collective-permute-start.1 = (bf16[4,4,256,128]{3,2,1,0:T(8,128)(2,1)S(1)}, bf16[4,4,256,128]{3,2,1,0:T(8,128)(2,1)S(1)}, u32[]{:S(2)}, u32[]{:S(2)}) collective-permute-start(bf16[4,4,256,128]{3,2,1,0:T(8,128)(2,1)S(1)} %all-to-all-done.3.own), channel_id=1, source_target_pairs={{0,16},{16,0},{1,17},{17,1},{2,18},{18,2},{3,19},{19,3},{4,20},{20... | collective-permute-start | bytes 3145736 | tf_op jit(solution)/shard_map/ppermute | solution.py:312
  77.5 10.4 %all-to-all-start.2 = ((bf16[4,128,256]{2,1,0:T(8,128)(2,1)}), bf16[4,128,256]{2,1,0:T(8,128)(2,1)S(1)}, u32[]{:S(2)}, u32[]{:S(2)}) async-start(bf16[4,128,256]{2,1,0:T(8,128)(2,1)} %get-tuple-element.30), calls=%async_computation.2 | async-start | bytes 524288 | tf_op jit(solution)/shard_map/all_to_all | solution.py:287
  89.4 12.8 %all-to-all-start.4 = ((bf16[4,128,512]{2,1,0:T(8,128)(2,1)}), bf16[4,128,512]{2,1,0:T(8,128)(2,1)S(1)}, u32[]{:S(2)}, u32[]{:S(2)}) async-start(bf16[4,128,512]{2,1,0:T(8,128)(2,1)} %shard_map.96), calls=%async_computation.4 | async-start | bytes 1048576 | tf_op jit(solution)/shard_map/all_to_all | solution.py:287
  94.1 3.2 %collective-permute-start.2 = (bf16[4,128,128]{2,1,0:T(8,128)(2,1)S(1)}, bf16[4,128,128]{2,1,0:T(8,128)(2,1)S(1)}, u32[]{:S(2)}, u32[]{:S(2)}) collective-permute-start(bf16[4,128,128]{2,1,0:T(8,128)(2,1)S(1)} %get-tuple-element.51), channel_id=1, source_target_pairs={{0,16},{16,0},{1,17},{17,1},{2,18},{18,2},{3,19},{19,3},{4,20},{20... | collective-permute-start | bytes 393224 | tf_op jit(solution)/shard_map/ppermute | solution.py:321
  103.6 10.2 %all-to-all-start.5 = ((bf16[4,128,256]{2,1,0:T(8,128)(2,1)}), bf16[4,128,256]{2,1,0:T(8,128)(2,1)S(1)}, u32[]{:S(2)}, u32[]{:S(2)}) async-start(bf16[4,128,256]{2,1,0:T(8,128)(2,1)} %get-tuple-element.33), calls=%async_computation.5 | async-start | bytes 524288 | tf_op jit(solution)/shard_map/all_to_all | solution.py:287
  107.0 35.7 %reduce-scatter.3.cloned.1.call-start = ((), (), s32[]{:S(2)}) async-start(), calls=%async_computation.13 | async-start | bytes 1310720 | tf_op jit(solution)/shard_map/reduce_scatter | solution.py:340
  107.0 3.2 %collective-permute-start.3 = (bf16[128,512]{1,0:T(8,128)(2,1)S(1)}, bf16[128,512]{1,0:T(8,128)(2,1)S(1)}, u32[]{:S(2)}, u32[]{:S(2)}) collective-permute-start(bf16[128,512]{1,0:T(8,128)(2,1)S(1)} %get-tuple-element.35.inner), channel_id=1, source_target_pairs={{0,16},{16,0},{1,17},{17,1},{2,18},{18,2},{3,19},{19,3},{4,20},{20... | collective-permute-start | bytes 393224 | tf_op jit(solution)/shard_map/ppermute | solution.py:332
  113.8 65.0 %reduce-scatter.5.cloned.1.call-start = ((), (), s32[]{:S(2)}) async-start(), calls=%async_computation.14 | async-start | bytes 327680 | tf_op jit(solution)/shard_map/reduce_scatter | solution.py:353
  125.9 15.5 %copy-start.2 = (f32[4,32,128]{2,1,0:T(8,128)S(1)}, f32[4,32,128]{2,1,0:T(8,128)}, u32[]{:S(2)}) copy-start(f32[4,32,128]{2,1,0:T(8,128)} %get-tuple-element.37.logit) | copy-start | bytes 196612
  126.0 15.4 %copy-start = (bf16[4,32,4096]{2,1,0:T(8,128)(2,1)S(1)}, bf16[4,32,4096]{2,1,0:T(8,128)(2,1)}, u32[]{:S(2)}) copy-start(bf16[4,32,4096]{2,1,0:T(8,128)(2,1)} %tok.3) | copy-start | bytes 3145732
  126.0 15.4 %copy-start.1 = (bf16[4,32,4096]{2,1,0:T(8,128)(2,1)S(1)}, bf16[4,32,4096]{2,1,0:T(8,128)(2,1)}, u32[]{:S(2)}) copy-start(bf16[4,32,4096]{2,1,0:T(8,128)(2,1)} %grd.1) | copy-start | bytes 3145732
  126.0 15.4 %copy-start.4 = (s32[4]{0:T(128)S(1)}, s32[4]{0:T(128)}, u32[]{:S(2)}) copy-start(s32[4]{0:T(128)} %get-tuple-element.27.kind) | copy-start | bytes 52
  141.4 15.0 %copy-start.3 = (bf16[4096,1]{0,1:T(2,128)(2,1)S(1)}, bf16[4096,1]{0,1:T(2,128)(2,1)}, u32[]{:S(2)}) copy-start(bf16[4096,1]{0,1:T(2,128)(2,1)} %param.9) | copy-start | bytes 24580
  169.9 3.1 %collective-permute-start.4 = (f32[8,512]{1,0:T(8,128)S(1)}, f32[8,512]{1,0:T(8,128)S(1)}, u32[]{:S(2)}, u32[]{:S(2)}) collective-permute-start(f32[8,512]{1,0:T(8,128)S(1)} %reduce_sum.18), channel_id=1, source_target_pairs={{0,16},{16,0},{1,17},{17,1},{2,18},{18,2},{3,19},{19,3},{4,20},{20... | collective-permute-start | bytes 49160 | tf_op jit(solution)/shard_map/ppermute | solution.py:362
  179.5 25.0 %all-to-all-start.10 = ((f32[16,8,512]{2,1,0:T(8,128)}), f32[16,8,512]{2,1,0:T(8,128)S(1)}, u32[]{:S(2)}, u32[]{:S(2)}) async-start(f32[16,8,512]{2,1,0:T(8,128)} %broadcast_in_dim.34), calls=%async_computation.12 | async-start | bytes 524288 | tf_op jit(solution)/shard_map/all_to_all | solution.py:287
  186.2 7.3 %collective-permute-start.5 = (bf16[256,128]{1,0:T(8,128)(2,1)}, bf16[256,128]{1,0:T(8,128)(2,1)S(1)}, u32[]{:S(2)}, u32[]{:S(2)}) collective-permute-start(bf16[256,128]{1,0:T(8,128)(2,1)} %reduce-scatter.5.cloned.1.call-done), channel_id=1, source_target_pairs={{0,0},{1,128},{2,256},{3,384},{128,1},{129,129},{130,257},{131,385... | collective-permute-start | bytes 196616 | tf_op jit(solution)/shard_map/ppermute | solution.py:365
Sparse Core Ops, SparseCore 0:
  113.9 22.7 reduce-scatter.2
  142.9 35.8 reduce-scatter.4

commit v4 on v3

--- a/solution.py
+++ b/solution.py
@@ -118,27 +118,29 @@
                     out[y, base + k * 32 : base + k * 32 + 32, o] = acc.astype(BF)
 
 
-def over_y_body(got, out):
+def over_y_body(at, got, *outs):
     stats = []
     for i in range(NY):
         rows = [got[i, 128:144, j * 128 : j * 128 + 128] for j in range(4)]
         stats.append(unpack_stats(jnp.concatenate(rows, 0)))
     top, factors, total = merge_stats(stats)
     packed = pack_stats(top, total)
-    for z in range(NL):
+    for step, out in enumerate(outs):
+        d = pl.ds(pl.multiple_of(lax.rem(at[0] + step, NL) * 256, 256), 256)
         for j in range(2):
-            out[z, 128:160, j * 128 : j * 128 + 128] = packed[j * 32 : j * 32 + 32]
+            out[128:160, j * 128 : j * 128 + 128] = packed[j * 32 : j * 32 + 32]
         for base in (0, 64):
-            acc = factors[0] * got[0, base : base + 64, z * 256 : z * 256 + 256].astype(F32)
+            acc = factors[0] * got[0, base : base + 64, d].astype(F32)
             for i in range(1, NY):
-                acc = acc + factors[i] * got[i, base : base + 64, z * 256 : z * 256 + 256].astype(F32)
-            out[z, base : base + 64, :] = acc.astype(BF)
-
-
-def over_zl_body(got, out, final):
+                acc = acc + factors[i] * got[i, base : base + 64, d].astype(F32)
+            out[base : base + 64, :] = acc.astype(BF)
+
+
+def over_zl_body(*refs):
+    got, out, final = refs[:NL], refs[NL], refs[NL + 1]
     stats = []
     for i in range(NL):
-        rows = [got[i, 128:160, j * 128 : j * 128 + 128] for j in range(2)]
+        rows = [got[i][128:160, j * 128 : j * 128 + 128] for j in range(2)]
         stats.append(unpack_stats(jnp.concatenate(rows, 0)))
     top, factors, total = merge_stats(stats)
     scale = 1.0 / total
@@ -146,9 +148,9 @@
     final[...] = jnp.where(lane == 0, top, total)
     factors = [f * scale for f in factors]
     for base in (0, 64):
-        acc = factors[0] * got[0, base : base + 64].astype(F32)
+        acc = factors[0] * got[0][base : base + 64].astype(F32)
         for i in range(1, NL):
-            acc = acc + factors[i] * got[i, base : base + 64].astype(F32)
+            acc = acc + factors[i] * got[i][base : base + 64].astype(F32)
         acc = acc.astype(BF)
         for z in range(NL):
             out[z, base : base + 64] = acc
@@ -308,14 +310,23 @@
     shard = lax.ppermute(shard, ("x", "y"), flip)
     sent, shard = lax.optimization_barrier((sent, shard))
     shard = lax.all_gather(shard, "zh", axis=0, tiled=False)
+    got = swap(sent, "y")
+    got, shard = lax.optimization_barrier((got, shard))
+
+    low = jnp.full((1,), lax.axis_index("zl"), jnp.int32)
+    parts = call(over_y_body, [sds((160, 256))] * NL, (got,), (low,), flops=1_000_000)
+    parts, shard = lax.optimization_barrier((parts, shard))
     shard = swap(jnp.broadcast_to(shard[None], (NX, NH, 256, 128)), "x")
+    parts = [parts[0]] + [
+        lax.ppermute(parts[i], "zl", [(z, (z + i) % NL) for z in range(NL)]) for i in range(1, NL)
+    ]
+    shard, parts = lax.optimization_barrier((shard, parts))
+    sent, final = call(
+        over_zl_body, [sds((NL, 128, 256)), sds((64, 128), F32)], tuple(parts), flops=300_000
+    )
+    sent, shard = lax.optimization_barrier((sent, shard))
+    mixed = swap(sent, "zl")
     other = lax.ppermute(shard, "core", cores)
-
-    sent = call(over_y_body, sds((NL, 160, 256)), (swap(sent, "y"),), flops=1_000_000)
-    sent, final = call(
-        over_zl_body, [sds((NL, 128, 256)), sds((64, 128), F32)], (swap(sent, "zl"),), flops=300_000
-    )
-    mixed = swap(sent, "zl")
     half = lax.dynamic_slice_in_dim(mixed, (1 - core) * 128, 128, axis=2)
     mixed_half = lax.dynamic_slice_in_dim(mixed, core * 128, 128, axis=2)
     mixed_other = lax.ppermute(half, "core", cores)
@@ -361,10 +372,11 @@
     droute = jnp.sum(swap(droute, ("x", "y")), axis=0)
     droute = droute + lax.ppermute(droute, "core", cores)
     droute, grads = lax.optimization_barrier((droute, grads))
-    droute = swap(jnp.broadcast_to(droute[None], (16, 8, 512)), ("zh", "zl"))
+    droute = lax.dynamic_slice_in_dim(droute, core * 4, 4, axis=0)
+    droute = swap(jnp.broadcast_to(droute[None], (16, 4, 512)), ("zh", "zl"))
     grads = lax.ppermute(grads, ("x", "y"), flip)
     droute, grads = lax.optimization_barrier((droute, grads))
-    droute = jnp.sum(droute, axis=0)
+    droute = lax.all_gather(jnp.sum(droute, axis=0), "core", axis=0, tiled=True)
     return grad_tokens, grads[None, :128], grads[None, 128:], droute.reshape(4096, 1)
 
 

time: 214 us -> 212 us (level)
  the two profiles are of different devices: /device:TPU:2 before, /device:TPU:1 now
where the time goes in v4:
time: 212 us; the launch traced here: 211 us
  blocking collectives  82.2 us (39%)
  starting transfers between devices  69.7 us (33%)
  waiting for transfers between devices  26.8 us (13%)
  between operations  14.2 us (7%)
  Pallas kernels  13.8 us (7%)
  local copies, waits for them, and re-layouts  3.3 us (2%)
    all_to_all x4, blocking collectives, swap(): return lax.all_to_all(value, axes, split_axis=0, concat_axis=0, tiled=True)  51.7 us
    all_to_all x6, starting transfers between devices, swap(): return lax.all_to_all(value, axes, split_axis=0, concat_axis=0, tiled=True)  33 us
    all_gather x1, blocking collectives, shards(): shard = lax.all_gather(shard, 'zh', axis=0, tiled=False)  25.2 us
    all_to_all x6, waiting for transfers between devices, swap(): return lax.all_to_all(value, axes, split_axis=0, concat_axis=0, tiled=True)  19.5 us
    pallas_call x9, Pallas kernels, call(): pl.pallas_call(body, out_shape=outs, in_specs=[sm] * len(smem_args) + [vm...  13.8 us
    ppermute x3, starting transfers between devices, shards(): lax.ppermute(parts[i], 'zl', [(z, (z + i) % NL) for z in range(NL)])  9.22 us
    ppermute x1, starting transfers between devices, shards(): other = lax.ppermute(shard, 'core', cores)  8.32 us
    ppermute x1, starting transfers between devices, shards(): droute = droute + lax.ppermute(droute, 'core', cores)  7.26 us
  transfers between devices with their start and end apart: 17, of which 9 were waited for; matrix products, arithmetic and copies ran while one was open for 0% of the time, Pallas kernels for 4%

profile of v4, /device:TPU:1, one launch (start us, length us, event | category | flops | bytes accessed | tf_op | source)
XLA Modules:
  0.0 210.9 jit_solution(11741320740963749691)
XLA Ops:
  8.6 4.2 %shard_map.93 = (bf16[4,144,1024]{2,1,0:T(8,128)(2,1)}, f32[4,32,128]{2,1,0:T(8,128)}, s32[4]{0:T(128)}) custom-call(s32[1]{0:T(128)} %bitcast.first, s32[1,64]{1,0:T(1,128)} %order.1, bf16[1,4096]{1,0:T(2,128)(2,1)} %bitcast.13, bf16[4,32,4096]{2,1,0:T(8,128)(2,1)} %tok.3, bf16[4,32,4096]{2,1,0:T(8,128)(2,1)} %grd.1), custom_call_target="tpu_custom_call" | custom-call | flops 10000000 | bytes 3350804 | tf_op jit(solution)/shard_map/pallas_call | solution.py:25
  12.8 9.4 %all-to-all-start = ((bf16[4,144,1024]{2,1,0:T(8,128)(2,1)}), bf16[4,144,1024]{2,1,0:T(8,128)(2,1)S(1)}, u32[]{:S(2)}, u32[]{:S(2)}) async-start(bf16[4,144,1024]{2,1,0:T(8,128)(2,1)} %get-tuple-element.47), calls=%async_computation | async-start | bytes 2359296 | tf_op jit(solution)/shard_map/all_to_all | solution.py:289
  22.2 25.2 %all-gather = bf16[1024,128]{1,0:T(8,128)(2,1)S(1)} all-gather(bf16[256,128]{1,0:T(8,128)(2,1)S(1)} %collective-permute-done), channel_id=2, replica_groups=mesh['x'=4,'zh'=4,'core'=2,'zl'=4,'y'=4] {'zh'}, dimensions={0}, use_global_device_ids=true | all-gather | bytes 327680 | tf_op jit(solution)/shard_map/all_gather | solution.py:312
  47.8 1.2 broadcast_in_dim.36
  49.0 3.5 %all-to-all-start.1 = ((bf16[4,4,256,128]{3,2,1,0:T(8,128)(2,1)}), bf16[4,4,256,128]{3,2,1,0:T(8,128)(2,1)S(1)}, u32[]{:S(2)}, u32[]{:S(2)}) async-start(bf16[4,4,256,128]{3,2,1,0:T(8,128)(2,1)} %broadcast_in_dim.36), calls=%async_computation.1 | async-start | bytes 2097152 | tf_op jit(solution)/shard_map/all_to_all | solution.py:289
  52.5 2.7 %collective-permute-start.1 = (bf16[160,256]{1,0:T(8,128)(2,1)S(1)}, bf16[160,256]{1,0:T(8,128)(2,1)S(1)}, u32[]{:S(2)}, u32[]{:S(2)}) collective-permute-start(bf16[160,256]{1,0:T(8,128)(2,1)S(1)} %get-tuple-element.57), channel_id=1, source_target_pairs={{0,4},{4,8},{8,12},{12,0},{1,5},{5,9},{9,13},{13,1},{2,6},{6,10},{... | collective-permute-start | bytes 245768 | tf_op jit(solution)/shard_map/ppermute | solution.py:321
  55.2 3.0 %collective-permute-start.2 = (bf16[160,256]{1,0:T(8,128)(2,1)S(1)}, bf16[160,256]{1,0:T(8,128)(2,1)S(1)}, u32[]{:S(2)}, u32[]{:S(2)}) collective-permute-start(bf16[160,256]{1,0:T(8,128)(2,1)S(1)} %get-tuple-element.58), channel_id=1, source_target_pairs={{0,8},{4,12},{8,0},{12,4},{1,9},{5,13},{9,1},{13,5},{2,10},{6,14},... | collective-permute-start | bytes 245768 | tf_op jit(solution)/shard_map/ppermute | solution.py:321
  58.2 3.6 %collective-permute-start.3 = (bf16[160,256]{1,0:T(8,128)(2,1)S(1)}, bf16[160,256]{1,0:T(8,128)(2,1)S(1)}, u32[]{:S(2)}, u32[]{:S(2)}) collective-permute-start(bf16[160,256]{1,0:T(8,128)(2,1)S(1)} %get-tuple-element.59), channel_id=1, source_target_pairs={{0,12},{4,0},{8,4},{12,8},{1,13},{5,1},{9,5},{13,9},{2,14},{6,2},{... | collective-permute-start | bytes 245768 | tf_op jit(solution)/shard_map/ppermute | solution.py:321
  62.5 1.5 collective-permute-done.3.refs_3_
  64.9 8.3 %collective-permute-start.4 = (bf16[4,4,256,128]{3,2,1,0:T(8,128)(2,1)S(1)}, bf16[4,4,256,128]{3,2,1,0:T(8,128)(2,1)S(1)}, u32[]{:S(2)}, u32[]{:S(2)}) collective-permute-start(bf16[4,4,256,128]{3,2,1,0:T(8,128)(2,1)S(1)} %all-to-all-done.1.own), channel_id=1, source_target_pairs={{0,16},{16,0},{1,17},{17,1},{2,18},{18,2},{3,19},{19,3},{4,20},{20... | collective-permute-start | bytes 3145736 | tf_op jit(solution)/shard_map/ppermute | solution.py:329
  73.3 4.7 %all-to-all-start.2 = ((bf16[4,128,256]{2,1,0:T(8,128)(2,1)}), bf16[4,128,256]{2,1,0:T(8,128)(2,1)S(1)}, u32[]{:S(2)}, u32[]{:S(2)}) async-start(bf16[4,128,256]{2,1,0:T(8,128)(2,1)} %get-tuple-element.66), calls=%async_computation.2 | async-start | bytes 524288 | tf_op jit(solution)/shard_map/all_to_all | solution.py:289
  77.9 7.5 %all-to-all-done.2.mixed = bf16[4,128,256]{2,1,0:T(8,128)(2,1)S(1)} async-done(((bf16[4,128,256]{2,1,0:T(8,128)(2,1)}), bf16[4,128,256]{2,1,0:T(8,128)(2,1)S(1)}, u32[]{:S(2)}, u32[]{:S(2)}) %all-to-all-start.2) | async-done | bytes 262176 | tf_op jit(solution)/shard_map/all_to_all | solution.py:289
  85.4 1.5 shard_map.96
  86.9 4.3 %all-to-all-start.3 = ((bf16[4,128,512]{2,1,0:T(8,128)(2,1)}), bf16[4,128,512]{2,1,0:T(8,128)(2,1)S(1)}, u32[]{:S(2)}, u32[]{:S(2)}) async-start(bf16[4,128,512]{2,1,0:T(8,128)(2,1)} %shard_map.96), calls=%async_computation.3 | async-start | bytes 1048576 | tf_op jit(solution)/shard_map/all_to_all | solution.py:289
  91.3 4.5 %collective-permute-start.5 = (bf16[4,128,128]{2,1,0:T(8,128)(2,1)S(1)}, bf16[4,128,128]{2,1,0:T(8,128)(2,1)S(1)}, u32[]{:S(2)}, u32[]{:S(2)}) collective-permute-start(bf16[4,128,128]{2,1,0:T(8,128)(2,1)S(1)} %get-tuple-element.87), channel_id=1, source_target_pairs={{0,16},{16,0},{1,17},{17,1},{2,18},{18,2},{3,19},{19,3},{4,20},{20... | collective-permute-start | bytes 393224 | tf_op jit(solution)/shard_map/ppermute | solution.py:332
  96.8 1.4 all-to-all-done.3.got
  98.2 1.4 shard_map.97
  99.6 4.0 %all-to-all-start.4 = ((bf16[4,128,256]{2,1,0:T(8,128)(2,1)}), bf16[4,128,256]{2,1,0:T(8,128)(2,1)S(1)}, u32[]{:S(2)}, u32[]{:S(2)}) async-start(bf16[4,128,256]{2,1,0:T(8,128)(2,1)} %get-tuple-element.69), calls=%async_computation.4 | async-start | bytes 524288 | tf_op jit(solution)/shard_map/all_to_all | solution.py:289
  103.6 5.1 %collective-permute-start.6 = (bf16[128,512]{1,0:T(8,128)(2,1)S(1)}, bf16[128,512]{1,0:T(8,128)(2,1)S(1)}, u32[]{:S(2)}, u32[]{:S(2)}) collective-permute-start(bf16[128,512]{1,0:T(8,128)(2,1)S(1)} %get-tuple-element.71.inner), channel_id=1, source_target_pairs={{0,16},{16,0},{1,17},{17,1},{2,18},{18,2},{3,19},{19,3},{4,20},{20... | collective-permute-start | bytes 393224 | tf_op jit(solution)/shard_map/ppermute | solution.py:343
  109.7 1.4 shard_map.98
  111.3 11.0 %all_to_all.50 = bf16[4,128,256]{2,1,0:T(8,128)(2,1)S(1)} all-to-all(bf16[4,128,256]{2,1,0:T(8,128)(2,1)S(1)} %shard_map.99), channel_id=1, replica_groups=mesh['x'=4,'zh'=4,'core'=2,'zl'=4,'y'=4] {'zl'}, dimensions={0} | all-to-all | bytes 524288 | tf_op jit(solution)/shard_map/all_to_all | solution.py:289
  122.4 14.1 %all_to_all.51.back = bf16[4,4,128,256]{3,2,1,0:T(8,128)(2,1)S(1)} all-to-all(bf16[4,4,128,256]{3,2,1,0:T(8,128)(2,1)S(1)} %broadcast_in_dim.37), channel_id=1, replica_groups=mesh['x'=4,'zh'=4,'core'=2,'zl'=4,'y'=4] {'y'}, dimensions={0} | all-to-all | bytes 2097152 | tf_op jit(solution)/shard_map/all_to_all | solution.py:289
  136.5 1.3 shard_map.100
  137.8 14.9 %all_to_all.52.got = f32[16,8,128]{2,1,0:T(8,128)S(1)} all-to-all(f32[16,8,128]{2,1,0:T(8,128)S(1)} %get-tuple-element.78), channel_id=1, replica_groups=mesh['x'=4,'zh'=4,'core'=2,'zl'=4,'y'=4] {'zl','y'}, dimensions={0} | all-to-all | bytes 131072 | tf_op jit(solution)/shard_map/all_to_all | solution.py:289
  152.7 2.5 %shard_map.101 = (bf16[4,32,4096]{2,1,0:T(8,128)(2,1)}, f32[16,8,512]{2,1,0:T(8,128)S(1)}) custom-call(s32[4]{0:T(128)S(1)} %copy-done.4, bf16[4,32,4096]{2,1,0:T(8,128)(2,1)S(1)} %copy-done, bf16[4,4,128,256]{3,2,1,0:T(8,128)(2,1)S(1)} %all_to_all.51.back, f32[4,32,128]{2,1,0:T(8,128)S(1)} %copy-done.2, f32[64,128]{1,0:T(8,128)S(1)} %get-tuple-element.74.final, ...), custom_call_target="tpu_custom_call" | custom-call | flops 5000000 | bytes 3645456 | tf_op jit(solution)/shard_map/pallas_call | solution.py:25
  155.2 11.7 %all_to_all.53 = f32[16,8,512]{2,1,0:T(8,128)S(1)} all-to-all(f32[16,8,512]{2,1,0:T(8,128)S(1)} %get-tuple-element.80), channel_id=1, replica_groups=mesh['x'=4,'zh'=4,'core'=2,'zl'=4,'y'=4] {'x','y'}, dimensions={0} | all-to-all | bytes 524288 | tf_op jit(solution)/shard_map/all_to_all | solution.py:289
  167.0 7.3 %collective-permute-start.7 = (f32[8,512]{1,0:T(8,128)S(1)}, f32[8,512]{1,0:T(8,128)S(1)}, u32[]{:S(2)}, u32[]{:S(2)}) collective-permute-start(f32[8,512]{1,0:T(8,128)S(1)} %reduce_sum.18), channel_id=1, source_target_pairs={{0,16},{16,0},{1,17},{17,1},{2,18},{18,2},{3,19},{19,3},{4,20},{20... | collective-permute-start | bytes 49160 | tf_op jit(solution)/shard_map/ppermute | solution.py:373
  175.1 2.4 %reduce-scatter.5.cloned.1.call-done = bf16[256,128]{1,0:T(8,128)(2,1)} async-done(((bf16[1024,128]{1,0:T(8,128)(2,1)}), bf16[256,128]{1,0:T(8,128)(2,1)}) %reduce-scatter.5.cloned.1.call-update) | async-done | bytes 65552 | tf_op jit(solution)/shard_map/reduce_scatter | solution.py:364
  178.1 7.2 %all-to-all-start.9 = ((f32[16,4,512]{2,1,0:T(4,128)}), f32[16,4,512]{2,1,0:T(4,128)S(1)}, u32[]{:S(2)}, u32[]{:S(2)}) async-start(f32[16,4,512]{2,1,0:T(4,128)} %broadcast_in_dim.38), calls=%async_computation.11 | async-start | bytes 262144 | tf_op jit(solution)/shard_map/all_to_all | solution.py:289
  185.3 1.5 collective-permute-start.8
  186.8 10.6 %all-to-all-done.9 = f32[16,4,512]{2,1,0:T(4,128)S(1)} async-done(((f32[16,4,512]{2,1,0:T(4,128)}), f32[16,4,512]{2,1,0:T(4,128)S(1)}, u32[]{:S(2)}, u32[]{:S(2)}) %all-to-all-start.9) | async-done | bytes 131104 | tf_op jit(solution)/shard_map/all_to_all | solution.py:289
  198.1 5.3 %all-gather.1 = f32[2,4,512]{2,1,0:T(4,128)S(1)} all-gather(f32[1,4,512]{2,1,0:T(4,128)S(1)} %bitcast.16), channel_id=1, replica_groups=mesh['x'=4,'zh'=4,'core'=2,'zl'=4,'y'=4] {'core'}, dimensions={0}, use_global_device_ids=true | all-gather | bytes 24576 | tf_op jit(solution)/shard_map/all_gather | solution.py:379
  (40 shorter events, 8.6 us)
Async XLA Ops:
  7.9 4.9 %collective-permute-start = (bf16[256,128]{1,0:T(8,128)(2,1)S(1)}, bf16[256,128]{1,0:T(8,128)(2,1)S(1)}, u32[]{:S(2)}, u32[]{:S(2)}) collective-permute-start(bf16[256,128]{1,0:T(8,128)(2,1)S(1)} %pad_maximum_fusion), channel_id=1, source_target_pairs={{0,0},{1,128},{2,256},{3,384},{128,1},{129,129},{130,257},{131,385... | collective-permute-start | bytes 196616 | tf_op jit(solution)/shard_map/ppermute | solution.py:310
  12.8 34.6 %all-to-all-start = ((bf16[4,144,1024]{2,1,0:T(8,128)(2,1)}), bf16[4,144,1024]{2,1,0:T(8,128)(2,1)S(1)}, u32[]{:S(2)}, u32[]{:S(2)}) async-start(bf16[4,144,1024]{2,1,0:T(8,128)(2,1)} %get-tuple-element.47), calls=%async_computation | async-start | bytes 2359296 | tf_op jit(solution)/shard_map/all_to_all | solution.py:289
  49.0 14.9 %all-to-all-start.1 = ((bf16[4,4,256,128]{3,2,1,0:T(8,128)(2,1)}), bf16[4,4,256,128]{3,2,1,0:T(8,128)(2,1)S(1)}, u32[]{:S(2)}, u32[]{:S(2)}) async-start(bf16[4,4,256,128]{3,2,1,0:T(8,128)(2,1)} %broadcast_in_dim.36), calls=%async_computation.1 | async-start | bytes 2097152 | tf_op jit(solution)/shard_map/all_to_all | solution.py:289
  52.5 9.2 %collective-permute-start.1 = (bf16[160,256]{1,0:T(8,128)(2,1)S(1)}, bf16[160,256]{1,0:T(8,128)(2,1)S(1)}, u32[]{:S(2)}, u32[]{:S(2)}) collective-permute-start(bf16[160,256]{1,0:T(8,128)(2,1)S(1)} %get-tuple-element.57), channel_id=1, source_target_pairs={{0,4},{4,8},{8,12},{12,0},{1,5},{5,9},{9,13},{13,1},{2,6},{6,10},{... | collective-permute-start | bytes 245768 | tf_op jit(solution)/shard_map/ppermute | solution.py:321
  55.2 7.3 %collective-permute-start.2 = (bf16[160,256]{1,0:T(8,128)(2,1)S(1)}, bf16[160,256]{1,0:T(8,128)(2,1)S(1)}, u32[]{:S(2)}, u32[]{:S(2)}) collective-permute-start(bf16[160,256]{1,0:T(8,128)(2,1)S(1)} %get-tuple-element.58), channel_id=1, source_target_pairs={{0,8},{4,12},{8,0},{12,4},{1,9},{5,13},{9,1},{13,5},{2,10},{6,14},... | collective-permute-start | bytes 245768 | tf_op jit(solution)/shard_map/ppermute | solution.py:321
  58.2 5.7 %collective-permute-start.3 = (bf16[160,256]{1,0:T(8,128)(2,1)S(1)}, bf16[160,256]{1,0:T(8,128)(2,1)S(1)}, u32[]{:S(2)}, u32[]{:S(2)}) collective-permute-start(bf16[160,256]{1,0:T(8,128)(2,1)S(1)} %get-tuple-element.59), channel_id=1, source_target_pairs={{0,12},{4,0},{8,4},{12,8},{1,13},{5,1},{9,5},{13,9},{2,14},{6,2},{... | collective-permute-start | bytes 245768 | tf_op jit(solution)/shard_map/ppermute | solution.py:321
  64.9 20.5 %collective-permute-start.4 = (bf16[4,4,256,128]{3,2,1,0:T(8,128)(2,1)S(1)}, bf16[4,4,256,128]{3,2,1,0:T(8,128)(2,1)S(1)}, u32[]{:S(2)}, u32[]{:S(2)}) collective-permute-start(bf16[4,4,256,128]{3,2,1,0:T(8,128)(2,1)S(1)} %all-to-all-done.1.own), channel_id=1, source_target_pairs={{0,16},{16,0},{1,17},{17,1},{2,18},{18,2},{3,19},{19,3},{4,20},{20... | collective-permute-start | bytes 3145736 | tf_op jit(solution)/shard_map/ppermute | solution.py:329
  73.3 12.2 %all-to-all-start.2 = ((bf16[4,128,256]{2,1,0:T(8,128)(2,1)}), bf16[4,128,256]{2,1,0:T(8,128)(2,1)S(1)}, u32[]{:S(2)}, u32[]{:S(2)}) async-start(bf16[4,128,256]{2,1,0:T(8,128)(2,1)} %get-tuple-element.66), calls=%async_computation.2 | async-start | bytes 524288 | tf_op jit(solution)/shard_map/all_to_all | solution.py:289
  86.9 11.3 %all-to-all-start.3 = ((bf16[4,128,512]{2,1,0:T(8,128)(2,1)}), bf16[4,128,512]{2,1,0:T(8,128)(2,1)S(1)}, u32[]{:S(2)}, u32[]{:S(2)}) async-start(bf16[4,128,512]{2,1,0:T(8,128)(2,1)} %shard_map.96), calls=%async_computation.3 | async-start | bytes 1048576 | tf_op jit(solution)/shard_map/all_to_all | solution.py:289
  91.3 5.5 %collective-permute-start.5 = (bf16[4,128,128]{2,1,0:T(8,128)(2,1)S(1)}, bf16[4,128,128]{2,1,0:T(8,128)(2,1)S(1)}, u32[]{:S(2)}, u32[]{:S(2)}) collective-permute-start(bf16[4,128,128]{2,1,0:T(8,128)(2,1)S(1)} %get-tuple-element.87), channel_id=1, source_target_pairs={{0,16},{16,0},{1,17},{17,1},{2,18},{18,2},{3,19},{19,3},{4,20},{20... | collective-permute-start | bytes 393224 | tf_op jit(solution)/shard_map/ppermute | solution.py:332
  99.6 11.5 %all-to-all-start.4 = ((bf16[4,128,256]{2,1,0:T(8,128)(2,1)}), bf16[4,128,256]{2,1,0:T(8,128)(2,1)S(1)}, u32[]{:S(2)}, u32[]{:S(2)}) async-start(bf16[4,128,256]{2,1,0:T(8,128)(2,1)} %get-tuple-element.69), calls=%async_computation.4 | async-start | bytes 524288 | tf_op jit(solution)/shard_map/all_to_all | solution.py:289
  103.6 34.2 %reduce-scatter.3.cloned.1.call-start = ((), (), s32[]{:S(2)}) async-start(), calls=%async_computation.12 | async-start | bytes 1310720 | tf_op jit(solution)/shard_map/reduce_scatter | solution.py:351
  103.6 6.1 %collective-permute-start.6 = (bf16[128,512]{1,0:T(8,128)(2,1)S(1)}, bf16[128,512]{1,0:T(8,128)(2,1)S(1)}, u32[]{:S(2)}, u32[]{:S(2)}) collective-permute-start(bf16[128,512]{1,0:T(8,128)(2,1)S(1)} %get-tuple-element.71.inner), channel_id=1, source_target_pairs={{0,16},{16,0},{1,17},{17,1},{2,18},{18,2},{3,19},{19,3},{4,20},{20... | collective-permute-start | bytes 393224 | tf_op jit(solution)/shard_map/ppermute | solution.py:343
  111.2 66.3 %reduce-scatter.5.cloned.1.call-start = ((), (), s32[]{:S(2)}) async-start(), calls=%async_computation.13 | async-start | bytes 327680 | tf_op jit(solution)/shard_map/reduce_scatter | solution.py:364
  122.3 14.2 %copy-start.2 = (f32[4,32,128]{2,1,0:T(8,128)S(1)}, f32[4,32,128]{2,1,0:T(8,128)}, u32[]{:S(2)}) copy-start(f32[4,32,128]{2,1,0:T(8,128)} %get-tuple-element.73.logit) | copy-start | bytes 196612
  122.4 14.1 %copy-start = (bf16[4,32,4096]{2,1,0:T(8,128)(2,1)S(1)}, bf16[4,32,4096]{2,1,0:T(8,128)(2,1)}, u32[]{:S(2)}) copy-start(bf16[4,32,4096]{2,1,0:T(8,128)(2,1)} %tok.3) | copy-start | bytes 3145732
  122.4 14.1 %copy-start.1 = (bf16[4,32,4096]{2,1,0:T(8,128)(2,1)S(1)}, bf16[4,32,4096]{2,1,0:T(8,128)(2,1)}, u32[]{:S(2)}) copy-start(bf16[4,32,4096]{2,1,0:T(8,128)(2,1)} %grd.1) | copy-start | bytes 3145732
  122.4 14.1 %copy-start.4 = (s32[4]{0:T(128)S(1)}, s32[4]{0:T(128)}, u32[]{:S(2)}) copy-start(s32[4]{0:T(128)} %get-tuple-element.45.kind) | copy-start | bytes 52
  136.5 16.2 %copy-start.3 = (bf16[4096,1]{0,1:T(2,128)(2,1)S(1)}, bf16[4096,1]{0,1:T(2,128)(2,1)}, u32[]{:S(2)}) copy-start(bf16[4096,1]{0,1:T(2,128)(2,1)} %param.9) | copy-start | bytes 24580
  167.0 8.1 %collective-permute-start.7 = (f32[8,512]{1,0:T(8,128)S(1)}, f32[8,512]{1,0:T(8,128)S(1)}, u32[]{:S(2)}, u32[]{:S(2)}) collective-permute-start(f32[8,512]{1,0:T(8,128)S(1)} %reduce_sum.18), channel_id=1, source_target_pairs={{0,16},{16,0},{1,17},{17,1},{2,18},{18,2},{3,19},{19,3},{4,20},{20... | collective-permute-start | bytes 49160 | tf_op jit(solution)/shard_map/ppermute | solution.py:373
  178.1 19.3 %all-to-all-start.9 = ((f32[16,4,512]{2,1,0:T(4,128)}), f32[16,4,512]{2,1,0:T(4,128)S(1)}, u32[]{:S(2)}, u32[]{:S(2)}) async-start(f32[16,4,512]{2,1,0:T(4,128)} %broadcast_in_dim.38), calls=%async_computation.11 | async-start | bytes 262144 | tf_op jit(solution)/shard_map/all_to_all | solution.py:289
  185.3 1.5 collective-permute-start.8
Sparse Core Ops, SparseCore 0:
  111.3 26.0 reduce-scatter.2
  140.4 36.9 reduce-scatter.4

commit v5 on v4

--- a/solution.py
+++ b/solution.py
@@ -353,6 +353,8 @@
     sent = call(sum_four_body, sds((NL, 128, 256)), (got,), flops=300_000)
     sent = swap(sent, "zl")
     back = swap(jnp.broadcast_to(sent[None], (NY, NL, 128, 256)), "y")
+    back, grads = lax.optimization_barrier((back, grads))
+    grads = lax.psum_scatter(grads, "zh", scatter_dimension=0, tiled=True)
     sent, dmix = call(
         slope_body,
         [sds((16, 8, 128), F32), sds((4, 32, 128), F32)],
@@ -360,8 +362,6 @@
         (kind,),
         flops=5_000_000,
     )
-    sent, grads = lax.optimization_barrier((sent, grads))
-    grads = lax.psum_scatter(grads, "zh", scatter_dimension=0, tiled=True)
     grad_tokens, droute = call(
         final_body,
         [sds((4, 32, 4096)), sds((16, 8, 512), F32)],

time: 212 us -> 212 us (level)
  transfers between devices with their start and end apart: 17 -> 17, of which waited for: 9 -> 10; matrix products, arithmetic and copies ran while one was open for 0% -> 0% of each run, Pallas kernels for 4% -> 4%
where the time goes in v5:
time: 212 us; the launch traced here: 211 us
  blocking collectives  81.3 us (38%)
  starting transfers between devices  69.7 us (33%)
  waiting for transfers between devices  27.7 us (13%)
  between operations  14.3 us (7%)
  Pallas kernels  13.8 us (7%)
  local copies, waits for them, and re-layouts  3.3 us (2%)
    all_to_all x4, blocking collectives, swap(): return lax.all_to_all(value, axes, split_axis=0, concat_axis=0, tiled=True)  50.8 us
    all_to_all x6, starting transfers between devices, swap(): return lax.all_to_all(value, axes, split_axis=0, concat_axis=0, tiled=True)  33.1 us
    all_gather x1, blocking collectives, shards(): shard = lax.all_gather(shard, 'zh', axis=0, tiled=False)  25.2 us
    all_to_all x6, waiting for transfers between devices, swap(): return lax.all_to_all(value, axes, split_axis=0, concat_axis=0, tiled=True)  19.5 us
    pallas_call x9, Pallas kernels, call(): pl.pallas_call(body, out_shape=outs, in_specs=[sm] * len(smem_args) + [vm...  13.8 us
    ppermute x3, starting transfers between devices, shards(): lax.ppermute(parts[i], 'zl', [(z, (z + i) % NL) for z in range(NL)])  9.22 us
    ppermute x1, starting transfers between devices, shards(): other = lax.ppermute(shard, 'core', cores)  8.32 us
    ppermute x1, starting transfers between devices, shards(): droute = droute + lax.ppermute(droute, 'core', cores)  7.26 us
  transfers between devices with their start and end apart: 17, of which 10 were waited for; matrix products, arithmetic and copies ran while one was open for 0% of the time, Pallas kernels for 4%

profile of v5, /device:TPU:1, one launch (start us, length us, event | category | flops | bytes accessed | tf_op | source)
XLA Modules:
  0.0 210.9 jit_solution(9095824960899205316)
XLA Ops:
  8.6 4.2 %shard_map.93 = (bf16[4,144,1024]{2,1,0:T(8,128)(2,1)}, f32[4,32,128]{2,1,0:T(8,128)}, s32[4]{0:T(128)}) custom-call(s32[1]{0:T(128)} %bitcast.first, s32[1,64]{1,0:T(1,128)} %order.1, bf16[1,4096]{1,0:T(2,128)(2,1)} %bitcast.13, bf16[4,32,4096]{2,1,0:T(8,128)(2,1)} %tok.3, bf16[4,32,4096]{2,1,0:T(8,128)(2,1)} %grd.1), custom_call_target="tpu_custom_call" | custom-call | flops 10000000 | bytes 3350804 | tf_op jit(solution)/shard_map/pallas_call | solution.py:25
  12.8 9.4 %all-to-all-start = ((bf16[4,144,1024]{2,1,0:T(8,128)(2,1)}), bf16[4,144,1024]{2,1,0:T(8,128)(2,1)S(1)}, u32[]{:S(2)}, u32[]{:S(2)}) async-start(bf16[4,144,1024]{2,1,0:T(8,128)(2,1)} %get-tuple-element.47), calls=%async_computation | async-start | bytes 2359296 | tf_op jit(solution)/shard_map/all_to_all | solution.py:289
  22.2 25.2 %all-gather = bf16[1024,128]{1,0:T(8,128)(2,1)S(1)} all-gather(bf16[256,128]{1,0:T(8,128)(2,1)S(1)} %collective-permute-done), channel_id=2, replica_groups=mesh['x'=4,'zh'=4,'core'=2,'zl'=4,'y'=4] {'zh'}, dimensions={0}, use_global_device_ids=true | all-gather | bytes 327680 | tf_op jit(solution)/shard_map/all_gather | solution.py:312
  47.8 1.2 broadcast_in_dim.36
  49.0 3.5 %all-to-all-start.1 = ((bf16[4,4,256,128]{3,2,1,0:T(8,128)(2,1)}), bf16[4,4,256,128]{3,2,1,0:T(8,128)(2,1)S(1)}, u32[]{:S(2)}, u32[]{:S(2)}) async-start(bf16[4,4,256,128]{3,2,1,0:T(8,128)(2,1)} %broadcast_in_dim.36), calls=%async_computation.1 | async-start | bytes 2097152 | tf_op jit(solution)/shard_map/all_to_all | solution.py:289
  52.5 2.7 %collective-permute-start.1 = (bf16[160,256]{1,0:T(8,128)(2,1)S(1)}, bf16[160,256]{1,0:T(8,128)(2,1)S(1)}, u32[]{:S(2)}, u32[]{:S(2)}) collective-permute-start(bf16[160,256]{1,0:T(8,128)(2,1)S(1)} %get-tuple-element.57), channel_id=1, source_target_pairs={{0,4},{4,8},{8,12},{12,0},{1,5},{5,9},{9,13},{13,1},{2,6},{6,10},{... | collective-permute-start | bytes 245768 | tf_op jit(solution)/shard_map/ppermute | solution.py:321
  55.2 3.0 %collective-permute-start.2 = (bf16[160,256]{1,0:T(8,128)(2,1)S(1)}, bf16[160,256]{1,0:T(8,128)(2,1)S(1)}, u32[]{:S(2)}, u32[]{:S(2)}) collective-permute-start(bf16[160,256]{1,0:T(8,128)(2,1)S(1)} %get-tuple-element.58), channel_id=1, source_target_pairs={{0,8},{4,12},{8,0},{12,4},{1,9},{5,13},{9,1},{13,5},{2,10},{6,14},... | collective-permute-start | bytes 245768 | tf_op jit(solution)/shard_map/ppermute | solution.py:321
  58.2 3.6 %collective-permute-start.3 = (bf16[160,256]{1,0:T(8,128)(2,1)S(1)}, bf16[160,256]{1,0:T(8,128)(2,1)S(1)}, u32[]{:S(2)}, u32[]{:S(2)}) collective-permute-start(bf16[160,256]{1,0:T(8,128)(2,1)S(1)} %get-tuple-element.59), channel_id=1, source_target_pairs={{0,12},{4,0},{8,4},{12,8},{1,13},{5,1},{9,5},{13,9},{2,14},{6,2},{... | collective-permute-start | bytes 245768 | tf_op jit(solution)/shard_map/ppermute | solution.py:321
  62.5 1.5 collective-permute-done.3.refs_3_
  64.9 8.3 %collective-permute-start.4 = (bf16[4,4,256,128]{3,2,1,0:T(8,128)(2,1)S(1)}, bf16[4,4,256,128]{3,2,1,0:T(8,128)(2,1)S(1)}, u32[]{:S(2)}, u32[]{:S(2)}) collective-permute-start(bf16[4,4,256,128]{3,2,1,0:T(8,128)(2,1)S(1)} %all-to-all-done.1.own), channel_id=1, source_target_pairs={{0,16},{16,0},{1,17},{17,1},{2,18},{18,2},{3,19},{19,3},{4,20},{20... | collective-permute-start | bytes 3145736 | tf_op jit(solution)/shard_map/ppermute | solution.py:329
  73.3 4.7 %all-to-all-start.2 = ((bf16[4,128,256]{2,1,0:T(8,128)(2,1)}), bf16[4,128,256]{2,1,0:T(8,128)(2,1)S(1)}, u32[]{:S(2)}, u32[]{:S(2)}) async-start(bf16[4,128,256]{2,1,0:T(8,128)(2,1)} %get-tuple-element.66), calls=%async_computation.2 | async-start | bytes 524288 | tf_op jit(solution)/shard_map/all_to_all | solution.py:289
  77.9 7.5 %all-to-all-done.2.mixed = bf16[4,128,256]{2,1,0:T(8,128)(2,1)S(1)} async-done(((bf16[4,128,256]{2,1,0:T(8,128)(2,1)}), bf16[4,128,256]{2,1,0:T(8,128)(2,1)S(1)}, u32[]{:S(2)}, u32[]{:S(2)}) %all-to-all-start.2) | async-done | bytes 262176 | tf_op jit(solution)/shard_map/all_to_all | solution.py:289
  85.4 1.5 shard_map.96
  86.9 4.3 %all-to-all-start.3 = ((bf16[4,128,512]{2,1,0:T(8,128)(2,1)}), bf16[4,128,512]{2,1,0:T(8,128)(2,1)S(1)}, u32[]{:S(2)}, u32[]{:S(2)}) async-start(bf16[4,128,512]{2,1,0:T(8,128)(2,1)} %shard_map.96), calls=%async_computation.3 | async-start | bytes 1048576 | tf_op jit(solution)/shard_map/all_to_all | solution.py:289
  91.3 4.5 %collective-permute-start.5 = (bf16[4,128,128]{2,1,0:T(8,128)(2,1)S(1)}, bf16[4,128,128]{2,1,0:T(8,128)(2,1)S(1)}, u32[]{:S(2)}, u32[]{:S(2)}) collective-permute-start(bf16[4,128,128]{2,1,0:T(8,128)(2,1)S(1)} %get-tuple-element.87), channel_id=1, source_target_pairs={{0,16},{16,0},{1,17},{17,1},{2,18},{18,2},{3,19},{19,3},{4,20},{20... | collective-permute-start | bytes 393224 | tf_op jit(solution)/shard_map/ppermute | solution.py:332
  96.8 1.4 all-to-all-done.3.got
  98.2 1.4 shard_map.97
  99.6 4.0 %all-to-all-start.4 = ((bf16[4,128,256]{2,1,0:T(8,128)(2,1)}), bf16[4,128,256]{2,1,0:T(8,128)(2,1)S(1)}, u32[]{:S(2)}, u32[]{:S(2)}) async-start(bf16[4,128,256]{2,1,0:T(8,128)(2,1)} %get-tuple-element.69), calls=%async_computation.4 | async-start | bytes 524288 | tf_op jit(solution)/shard_map/all_to_all | solution.py:289
  103.6 5.1 %collective-permute-start.6 = (bf16[128,512]{1,0:T(8,128)(2,1)S(1)}, bf16[128,512]{1,0:T(8,128)(2,1)S(1)}, u32[]{:S(2)}, u32[]{:S(2)}) collective-permute-start(bf16[128,512]{1,0:T(8,128)(2,1)S(1)} %get-tuple-element.71.inner), channel_id=1, source_target_pairs={{0,16},{16,0},{1,17},{17,1},{2,18},{18,2},{3,19},{19,3},{4,20},{20... | collective-permute-start | bytes 393224 | tf_op jit(solution)/shard_map/ppermute | solution.py:343
  109.7 1.4 shard_map.98
  111.3 11.0 %all_to_all.50 = bf16[4,128,256]{2,1,0:T(8,128)(2,1)S(1)} all-to-all(bf16[4,128,256]{2,1,0:T(8,128)(2,1)S(1)} %shard_map.99), channel_id=1, replica_groups=mesh['x'=4,'zh'=4,'core'=2,'zl'=4,'y'=4] {'zl'}, dimensions={0} | all-to-all | bytes 524288 | tf_op jit(solution)/shard_map/all_to_all | solution.py:289
  122.5 14.1 %all_to_all.51.back = bf16[4,4,128,256]{3,2,1,0:T(8,128)(2,1)S(1)} all-to-all(bf16[4,4,128,256]{3,2,1,0:T(8,128)(2,1)S(1)} %broadcast_in_dim.37), channel_id=1, replica_groups=mesh['x'=4,'zh'=4,'core'=2,'zl'=4,'y'=4] {'y'}, dimensions={0} | all-to-all | bytes 2097152 | tf_op jit(solution)/shard_map/all_to_all | solution.py:289
  137.5 1.3 shard_map.100
  138.8 14.7 %all_to_all.52.got = f32[16,8,128]{2,1,0:T(8,128)S(1)} all-to-all(f32[16,8,128]{2,1,0:T(8,128)S(1)} %get-tuple-element.78), channel_id=1, replica_groups=mesh['x'=4,'zh'=4,'core'=2,'zl'=4,'y'=4] {'zl','y'}, dimensions={0} | all-to-all | bytes 131072 | tf_op jit(solution)/shard_map/all_to_all | solution.py:289
  153.5 2.5 %shard_map.101 = (bf16[4,32,4096]{2,1,0:T(8,128)(2,1)}, f32[16,8,512]{2,1,0:T(8,128)S(1)}) custom-call(s32[4]{0:T(128)S(1)} %copy-done.4, bf16[4,32,4096]{2,1,0:T(8,128)(2,1)S(1)} %copy-done, bf16[4,4,128,256]{3,2,1,0:T(8,128)(2,1)S(1)} %all_to_all.51.back, f32[4,32,128]{2,1,0:T(8,128)S(1)} %copy-done.2, f32[64,128]{1,0:T(8,128)S(1)} %get-tuple-element.76.final, ...), custom_call_target="tpu_custom_call" | custom-call | flops 5000000 | bytes 3645456 | tf_op jit(solution)/shard_map/pallas_call | solution.py:25
  156.0 11.0 %all_to_all.53 = f32[16,8,512]{2,1,0:T(8,128)S(1)} all-to-all(f32[16,8,512]{2,1,0:T(8,128)S(1)} %get-tuple-element.80), channel_id=1, replica_groups=mesh['x'=4,'zh'=4,'core'=2,'zl'=4,'y'=4] {'x','y'}, dimensions={0} | all-to-all | bytes 524288 | tf_op jit(solution)/shard_map/all_to_all | solution.py:289
  167.0 7.3 %collective-permute-start.7 = (f32[8,512]{1,0:T(8,128)S(1)}, f32[8,512]{1,0:T(8,128)S(1)}, u32[]{:S(2)}, u32[]{:S(2)}) collective-permute-start(f32[8,512]{1,0:T(8,128)S(1)} %reduce_sum.18), channel_id=1, source_target_pairs={{0,16},{16,0},{1,17},{17,1},{2,18},{18,2},{3,19},{19,3},{4,20},{20... | collective-permute-start | bytes 49160 | tf_op jit(solution)/shard_map/ppermute | solution.py:373
  175.1 2.4 %reduce-scatter.5.cloned.1.call-done = bf16[256,128]{1,0:T(8,128)(2,1)} async-done(((bf16[1024,128]{1,0:T(8,128)(2,1)}), bf16[256,128]{1,0:T(8,128)(2,1)}) %reduce-scatter.5.cloned.1.call-update) | async-done | bytes 65552 | tf_op jit(solution)/shard_map/reduce_scatter | solution.py:357
  178.2 7.2 %all-to-all-start.9 = ((f32[16,4,512]{2,1,0:T(4,128)}), f32[16,4,512]{2,1,0:T(4,128)S(1)}, u32[]{:S(2)}, u32[]{:S(2)}) async-start(f32[16,4,512]{2,1,0:T(4,128)} %broadcast_in_dim.38), calls=%async_computation.11 | async-start | bytes 262144 | tf_op jit(solution)/shard_map/all_to_all | solution.py:289
  185.4 1.5 collective-permute-start.8
  186.9 10.5 %all-to-all-done.9 = f32[16,4,512]{2,1,0:T(4,128)S(1)} async-done(((f32[16,4,512]{2,1,0:T(4,128)}), f32[16,4,512]{2,1,0:T(4,128)S(1)}, u32[]{:S(2)}, u32[]{:S(2)}) %all-to-all-start.9) | async-done | bytes 131104 | tf_op jit(solution)/shard_map/all_to_all | solution.py:289
  198.1 5.3 %all-gather.1 = f32[2,4,512]{2,1,0:T(4,128)S(1)} all-gather(f32[1,4,512]{2,1,0:T(4,128)S(1)} %bitcast.16), channel_id=1, replica_groups=mesh['x'=4,'zh'=4,'core'=2,'zl'=4,'y'=4] {'core'}, dimensions={0}, use_global_device_ids=true | all-gather | bytes 24576 | tf_op jit(solution)/shard_map/all_gather | solution.py:379
  (40 shorter events, 9.5 us)
Async XLA Ops:
  7.9 4.9 %collective-permute-start = (bf16[256,128]{1,0:T(8,128)(2,1)S(1)}, bf16[256,128]{1,0:T(8,128)(2,1)S(1)}, u32[]{:S(2)}, u32[]{:S(2)}) collective-permute-start(bf16[256,128]{1,0:T(8,128)(2,1)S(1)} %pad_maximum_fusion), channel_id=1, source_target_pairs={{0,0},{1,128},{2,256},{3,384},{128,1},{129,129},{130,257},{131,385... | collective-permute-start | bytes 196616 | tf_op jit(solution)/shard_map/ppermute | solution.py:310
  12.8 34.6 %all-to-all-start = ((bf16[4,144,1024]{2,1,0:T(8,128)(2,1)}), bf16[4,144,1024]{2,1,0:T(8,128)(2,1)S(1)}, u32[]{:S(2)}, u32[]{:S(2)}) async-start(bf16[4,144,1024]{2,1,0:T(8,128)(2,1)} %get-tuple-element.47), calls=%async_computation | async-start | bytes 2359296 | tf_op jit(solution)/shard_map/all_to_all | solution.py:289
  49.0 14.9 %all-to-all-start.1 = ((bf16[4,4,256,128]{3,2,1,0:T(8,128)(2,1)}), bf16[4,4,256,128]{3,2,1,0:T(8,128)(2,1)S(1)}, u32[]{:S(2)}, u32[]{:S(2)}) async-start(bf16[4,4,256,128]{3,2,1,0:T(8,128)(2,1)} %broadcast_in_dim.36), calls=%async_computation.1 | async-start | bytes 2097152 | tf_op jit(solution)/shard_map/all_to_all | solution.py:289
  52.5 9.2 %collective-permute-start.1 = (bf16[160,256]{1,0:T(8,128)(2,1)S(1)}, bf16[160,256]{1,0:T(8,128)(2,1)S(1)}, u32[]{:S(2)}, u32[]{:S(2)}) collective-permute-start(bf16[160,256]{1,0:T(8,128)(2,1)S(1)} %get-tuple-element.57), channel_id=1, source_target_pairs={{0,4},{4,8},{8,12},{12,0},{1,5},{5,9},{9,13},{13,1},{2,6},{6,10},{... | collective-permute-start | bytes 245768 | tf_op jit(solution)/shard_map/ppermute | solution.py:321
  55.2 7.3 %collective-permute-start.2 = (bf16[160,256]{1,0:T(8,128)(2,1)S(1)}, bf16[160,256]{1,0:T(8,128)(2,1)S(1)}, u32[]{:S(2)}, u32[]{:S(2)}) collective-permute-start(bf16[160,256]{1,0:T(8,128)(2,1)S(1)} %get-tuple-element.58), channel_id=1, source_target_pairs={{0,8},{4,12},{8,0},{12,4},{1,9},{5,13},{9,1},{13,5},{2,10},{6,14},... | collective-permute-start | bytes 245768 | tf_op jit(solution)/shard_map/ppermute | solution.py:321
  58.2 5.7 %collective-permute-start.3 = (bf16[160,256]{1,0:T(8,128)(2,1)S(1)}, bf16[160,256]{1,0:T(8,128)(2,1)S(1)}, u32[]{:S(2)}, u32[]{:S(2)}) collective-permute-start(bf16[160,256]{1,0:T(8,128)(2,1)S(1)} %get-tuple-element.59), channel_id=1, source_target_pairs={{0,12},{4,0},{8,4},{12,8},{1,13},{5,1},{9,5},{13,9},{2,14},{6,2},{... | collective-permute-start | bytes 245768 | tf_op jit(solution)/shard_map/ppermute | solution.py:321
  64.9 20.5 %collective-permute-start.4 = (bf16[4,4,256,128]{3,2,1,0:T(8,128)(2,1)S(1)}, bf16[4,4,256,128]{3,2,1,0:T(8,128)(2,1)S(1)}, u32[]{:S(2)}, u32[]{:S(2)}) collective-permute-start(bf16[4,4,256,128]{3,2,1,0:T(8,128)(2,1)S(1)} %all-to-all-done.1.own), channel_id=1, source_target_pairs={{0,16},{16,0},{1,17},{17,1},{2,18},{18,2},{3,19},{19,3},{4,20},{20... | collective-permute-start | bytes 3145736 | tf_op jit(solution)/shard_map/ppermute | solution.py:329
  73.3 12.2 %all-to-all-start.2 = ((bf16[4,128,256]{2,1,0:T(8,128)(2,1)}), bf16[4,128,256]{2,1,0:T(8,128)(2,1)S(1)}, u32[]{:S(2)}, u32[]{:S(2)}) async-start(bf16[4,128,256]{2,1,0:T(8,128)(2,1)} %get-tuple-element.66), calls=%async_computation.2 | async-start | bytes 524288 | tf_op jit(solution)/shard_map/all_to_all | solution.py:289
  86.9 11.3 %all-to-all-start.3 = ((bf16[4,128,512]{2,1,0:T(8,128)(2,1)}), bf16[4,128,512]{2,1,0:T(8,128)(2,1)S(1)}, u32[]{:S(2)}, u32[]{:S(2)}) async-start(bf16[4,128,512]{2,1,0:T(8,128)(2,1)} %shard_map.96), calls=%async_computation.3 | async-start | bytes 1048576 | tf_op jit(solution)/shard_map/all_to_all | solution.py:289
  91.3 5.5 %collective-permute-start.5 = (bf16[4,128,128]{2,1,0:T(8,128)(2,1)S(1)}, bf16[4,128,128]{2,1,0:T(8,128)(2,1)S(1)}, u32[]{:S(2)}, u32[]{:S(2)}) collective-permute-start(bf16[4,128,128]{2,1,0:T(8,128)(2,1)S(1)} %get-tuple-element.87), channel_id=1, source_target_pairs={{0,16},{16,0},{1,17},{17,1},{2,18},{18,2},{3,19},{19,3},{4,20},{20... | collective-permute-start | bytes 393224 | tf_op jit(solution)/shard_map/ppermute | solution.py:332
  99.6 11.5 %all-to-all-start.4 = ((bf16[4,128,256]{2,1,0:T(8,128)(2,1)}), bf16[4,128,256]{2,1,0:T(8,128)(2,1)S(1)}, u32[]{:S(2)}, u32[]{:S(2)}) async-start(bf16[4,128,256]{2,1,0:T(8,128)(2,1)} %get-tuple-element.69), calls=%async_computation.4 | async-start | bytes 524288 | tf_op jit(solution)/shard_map/all_to_all | solution.py:289
  103.6 33.8 %reduce-scatter.3.cloned.1.call-start = ((), (), s32[]{:S(2)}) async-start(), calls=%async_computation.12 | async-start | bytes 1310720 | tf_op jit(solution)/shard_map/reduce_scatter | solution.py:351
  103.6 6.1 %collective-permute-start.6 = (bf16[128,512]{1,0:T(8,128)(2,1)S(1)}, bf16[128,512]{1,0:T(8,128)(2,1)S(1)}, u32[]{:S(2)}, u32[]{:S(2)}) collective-permute-start(bf16[128,512]{1,0:T(8,128)(2,1)S(1)} %get-tuple-element.71.inner), channel_id=1, source_target_pairs={{0,16},{16,0},{1,17},{17,1},{2,18},{18,2},{3,19},{19,3},{4,20},{20... | collective-permute-start | bytes 393224 | tf_op jit(solution)/shard_map/ppermute | solution.py:343
  111.2 66.3 %reduce-scatter.5.cloned.1.call-start = ((), (), s32[]{:S(2)}) async-start(), calls=%async_computation.13 | async-start | bytes 327680 | tf_op jit(solution)/shard_map/reduce_scatter | solution.py:357
  122.4 15.0 %copy-start = (bf16[4,32,4096]{2,1,0:T(8,128)(2,1)S(1)}, bf16[4,32,4096]{2,1,0:T(8,128)(2,1)}, u32[]{:S(2)}) copy-start(bf16[4,32,4096]{2,1,0:T(8,128)(2,1)} %tok.3) | copy-start | bytes 3145732
  122.4 15.0 %copy-start.1 = (bf16[4,32,4096]{2,1,0:T(8,128)(2,1)S(1)}, bf16[4,32,4096]{2,1,0:T(8,128)(2,1)}, u32[]{:S(2)}) copy-start(bf16[4,32,4096]{2,1,0:T(8,128)(2,1)} %grd.1) | copy-start | bytes 3145732
  122.4 15.0 %copy-start.2 = (f32[4,32,128]{2,1,0:T(8,128)S(1)}, f32[4,32,128]{2,1,0:T(8,128)}, u32[]{:S(2)}) copy-start(f32[4,32,128]{2,1,0:T(8,128)} %get-tuple-element.75.logit) | copy-start | bytes 196612
  122.4 15.0 %copy-start.4 = (s32[4]{0:T(128)S(1)}, s32[4]{0:T(128)}, u32[]{:S(2)}) copy-start(s32[4]{0:T(128)} %get-tuple-element.45.kind) | copy-start | bytes 52
  137.5 16.0 %copy-start.3 = (bf16[4096,1]{0,1:T(2,128)(2,1)S(1)}, bf16[4096,1]{0,1:T(2,128)(2,1)}, u32[]{:S(2)}) copy-start(bf16[4096,1]{0,1:T(2,128)(2,1)} %param.9) | copy-start | bytes 24580
  167.0 8.1 %collective-permute-start.7 = (f32[8,512]{1,0:T(8,128)S(1)}, f32[8,512]{1,0:T(8,128)S(1)}, u32[]{:S(2)}, u32[]{:S(2)}) collective-permute-start(f32[8,512]{1,0:T(8,128)S(1)} %reduce_sum.18), channel_id=1, source_target_pairs={{0,16},{16,0},{1,17},{17,1},{2,18},{18,2},{3,19},{19,3},{4,20},{20... | collective-permute-start | bytes 49160 | tf_op jit(solution)/shard_map/ppermute | solution.py:373
  178.2 19.3 %all-to-all-start.9 = ((f32[16,4,512]{2,1,0:T(4,128)}), f32[16,4,512]{2,1,0:T(4,128)S(1)}, u32[]{:S(2)}, u32[]{:S(2)}) async-start(f32[16,4,512]{2,1,0:T(4,128)} %broadcast_in_dim.38), calls=%async_computation.11 | async-start | bytes 262144 | tf_op jit(solution)/shard_map/all_to_all | solution.py:289
  185.4 1.5 collective-permute-start.8
Sparse Core Ops, SparseCore 0:
  111.3 26.0 reduce-scatter.2
  140.4 37.0 reduce-scatter.4
